TPU v7x, 256 devices: a whole 4x4x8 slice. The times are simulated.
256 devices in a mesh: pos: 8 (over z), ch: 32 (over x, y, core).
Axes of the slice: x: 4, y: 4, z: 8, core: 2. Of those that a mesh axis runs over, the one named last changes fastest.
Arguments:
- queries: bfloat16 [8192, 4096], P('pos', 'ch'), may hold values from -6 to 6
- keys: bfloat16 [8192, 4096], P('pos', 'ch'), may hold values from -6 to 6
- values: bfloat16 [8192, 4096], P('pos', 'ch'), may hold values from -6 to 6
- residue: float32 [4096, 16], P('ch'), may hold values from -0.125 to 0.125
- rate: float32 [4096, 16], P('ch'), may hold values from 6.1035156e-05 to 0.1
- skip: float32 [4096], P('ch'), may hold values from -1 to 1
- w_out: bfloat16 [4096, 4096], P('ch'), may hold values from -0.1875 to 0.1875
- lengths: int32 [3], replicated, may hold values from 1 to 4, 8 in all
- d_out: bfloat16 [8192, 4096], P('pos', 'ch'), may hold values from -6 to 6
Outputs:
- out: bfloat16 [8192, 4096], P('pos', 'ch')
- d_queries: bfloat16 [8192, 4096], P('pos', 'ch')
- d_keys: bfloat16 [8192, 4096], P('pos', 'ch')
- d_values: bfloat16 [8192, 4096], P('pos', 'ch')
- d_residue: float32 [4096, 16], P('ch')
- d_rate: float32 [4096, 16], P('ch')
- d_skip: float32 [4096], P('ch')
- d_w_out: float32 [4096, 4096], P('ch')
Inputs may be any that keep to these rules, and one draw needn't show every extreme that they name: `lengths`: lengths count whole blocks of 1024 positions and add up to 8; the longest document has exactly 4 blocks.
All inputs are finite; a program needn't handle non-finite values.
Results may differ from a plain program's by a relative error of at most 0.023.
Values may be sent and summed in bfloat16 or wider, within the bound.
A program may use at most 128 MiB of HBM per device.

v0:
```python
import jax
import jax.numpy as jnp
from jax import lax
from jax.sharding import PartitionSpec as P

SUB = 128


highest = lax.Precision.HIGHEST


def carried_in(part, axis, combine, identity, reverse):
    count = lax.axis_size(axis)
    place = lax.axis_index(axis)
    ahead = count - 1 - place if reverse else place
    gathered = jax.tree.map(lambda a: lax.all_gather(a, axis), part)
    state = jax.tree.map(lambda a, e: jnp.zeros_like(a) + jnp.asarray(e, a.dtype), part, identity)

    def one(turn, state):
        source = count - 1 - turn if reverse else turn
        return combine(
            state, jax.tree.map(lambda a: lax.dynamic_index_in_dim(a, source, 0, False), gathered)
        )

    return lax.fori_loop(0, ahead, one, state)


def device_state(blocks, rate):
    pieces = blocks.shape[0]
    lag_steps = jnp.arange(SUB).astype(jnp.float32)
    tail_decay = jnp.exp(-rate[:, :, None] * (SUB - lag_steps)[None, None, :])
    end_states = jnp.einsum("dms,nsd->nmd", tail_decay, blocks, precision=highest)
    span_index = jnp.arange(pieces).astype(jnp.float32)
    weight = jnp.exp(-rate.T[None, :, :] * SUB * (pieces - 1 - span_index)[:, None, None])
    summary = jnp.sum(end_states * weight, axis=0)
    through = jnp.exp(-rate.T * (SUB * pieces))
    return (through, summary)


def device_output(blocks, residue, rate, skip, entering):
    pieces = blocks.shape[0]
    lag_steps = jnp.arange(SUB).astype(jnp.float32)
    powers = jnp.exp(-rate[:, :, None] * lag_steps[None, None, :])
    kernel = jnp.einsum("dm,dmj->dj", residue, powers, precision=highest)
    lag_grid = jnp.arange(SUB)[:, None] - jnp.arange(SUB)[None, :]
    toeplitz = jnp.where(
        lag_grid[None] >= 0, jnp.take(kernel, jnp.clip(lag_grid, 0, SUB - 1), axis=1), 0.0
    )
    intra_part = jnp.einsum("dts,nsd->ntd", toeplitz, blocks, precision=highest)
    tail_decay = jnp.exp(-rate[:, :, None] * (SUB - lag_steps)[None, None, :])
    end_states = jnp.einsum("dms,nsd->nmd", tail_decay, blocks, precision=highest)
    sub_decay = jnp.exp(-rate * SUB).T
    carried = entering
    inflow = []
    for piece_id in range(pieces):
        inflow.append(carried)
        carried = carried * sub_decay + end_states[piece_id]
    entering_all = jnp.stack(inflow, axis=0)
    head_decay = residue[:, :, None] * powers
    cross_part = jnp.einsum("dmt,nmd->ntd", head_decay, entering_all, precision=highest)
    chan_width = blocks.shape[2]
    mixed_in = blocks.reshape(-1, chan_width)
    return (intra_part + cross_part).reshape(-1, chan_width) + skip[None, :] * mixed_in


def chain(earlier, later):
    return (earlier[0] * later[0], earlier[1] * later[0] + later[1])


def shards(queries, keys, values, residue, rate, skip, w_out, lengths, d_out):
    tok_rows, chan_width = queries.shape
    pieces = tok_rows // SUB
    query_full = queries.astype(jnp.float32)
    key_full = keys.astype(jnp.float32)
    value_full = values.astype(jnp.float32)
    mixed_in = key_full * value_full
    blocks = mixed_in.reshape(pieces, SUB, chan_width)
    position = lax.axis_index("pos")
    begins = jnp.cumsum(lengths) - lengths
    keep_flag = jnp.where(jnp.any(begins == position), 0.0, 1.0).astype(jnp.float32)
    (through, summary), pull_state = jax.vjp(device_state, blocks, rate)
    gate_vals = through * keep_flag
    arriving = carried_in(
        (gate_vals, summary),
        "pos",
        chain,
        (jnp.ones_like(gate_vals), jnp.zeros_like(summary)),
        False,
    )[1]
    entering = arriving * keep_flag
    conv_field, pull_out = jax.vjp(device_output, blocks, residue, rate, skip, entering)
    product = (query_full * conv_field).astype(jnp.bfloat16)
    w_part = w_out
    result = (
        lax.psum_scatter(
            lax.dot_general(
                w_part, product, (((0,), (1,)), ((), ())), preferred_element_type=jnp.float32
            ).astype(jnp.bfloat16),
            "ch",
            scatter_dimension=0,
            tiled=True,
        )
        .astype(jnp.float32)
        .T.astype(jnp.bfloat16)
    )
    shard_piece = lax.all_gather(d_out, "ch", axis=1, tiled=True)
    w_part = w_out
    d_prod = lax.dot_general(
        shard_piece, w_part, (((1,), (1,)), ((), ())), preferred_element_type=jnp.float32
    )
    w_block = lax.dot_general(
        product, shard_piece, (((0,), (0,)), ((), ())), preferred_element_type=jnp.float32
    )
    d_weight = w_block
    d_product, d_weight = (d_prod, d_weight)
    d_field = d_product * query_full
    d_queries = (d_product * conv_field).astype(jnp.bfloat16)
    d_blocks, d_residue, d_rate, d_skip, d_entering = pull_out(d_field)
    adjoint = d_entering * keep_flag
    later_adj = carried_in(
        (gate_vals, adjoint),
        "pos",
        chain,
        (jnp.ones_like(gate_vals), jnp.zeros_like(adjoint)),
        True,
    )[1]
    d_blocks_state, d_rate_state = pull_state((later_adj * arriving * keep_flag, later_adj))
    d_mixed = (d_blocks + d_blocks_state).reshape(tok_rows, chan_width)
    d_keys = (d_mixed * value_full).astype(jnp.bfloat16)
    d_values = (d_mixed * key_full).astype(jnp.bfloat16)
    param_sums = (
        lax.psum(d_residue.astype(jnp.bfloat16), "pos").astype(jnp.float32),
        lax.psum((d_rate + d_rate_state).astype(jnp.bfloat16), "pos").astype(jnp.float32),
        lax.psum(d_skip.astype(jnp.bfloat16), "pos").astype(jnp.float32),
        lax.psum(d_weight.astype(jnp.bfloat16), "pos").astype(jnp.float32),
    )
    return (
        result,
        d_queries,
        d_keys,
        d_values,
        param_sums[0],
        param_sums[1],
        param_sums[2],
        param_sums[3],
    )


def solution(mesh):
    in_specs = (
        P("pos", "ch"),
        P("pos", "ch"),
        P("pos", "ch"),
        P("ch", None),
        P("ch", None),
        P("ch"),
        P("ch", None),
        P(),
        P("pos", "ch"),
    )
    out_specs = (
        P("pos", "ch"),
        P("pos", "ch"),
        P("pos", "ch"),
        P("pos", "ch"),
        P("ch", None),
        P("ch", None),
        P("ch"),
        P("ch", None),
    )
    return jax.shard_map(shards, mesh=mesh, in_specs=in_specs, out_specs=out_specs, check_vma=False)
```

profile of v0, /device:TPU:1, one launch (start us, length us, event | category | flops | bytes accessed | tf_op | source)
XLA Modules:
  0.0 608.7 jit_solution(2853176529215634406)
XLA Ops:
  15.6 63.6 %all-gather.5.cloned.1.call-done = bf16[1024,4096]{1,0:T(8,128)(2,1)} async-done(((bf16[1024,128]{1,0:T(8,128)(2,1)}), bf16[1024,4096]{1,0:T(8,128)(2,1)}) %all-gather.5.cloned.1.call-update) | async-done | bytes 8388624 | tf_op jit(solution)/shard_map/all_gather | solution.py:106
  79.3 7.1 %multiply_reduce_fusion.1 = (bf16[128]{0:T(256)(128)(2,1)}, f32[1024,128]{1,0:T(8,128)S(1)}, f32[1024,128]{1,0:T(8,128)S(1)}, f32[1024,128]{1,0:T(8,128)}) fusion(bf16[1024,128]{1,0:T(8,128)(2,1)} %param.15, bf16[1024,128]{1,0:T(8,128)(2,1)} %param.14, bf16[1024,128]{1,0:T(8,128)(2,1)} %param.13, bf16[1024,4096]{1,0:T(8,128)(2,1)} %all-gather.5.cloned.1.call-done, ...), kind=kOutput, calls=%fused_computation.53 | convolution fusion | flops 1074659200 | bytes 11796736 | tf_op jit(solution)/shard_map/dot_general | solution.py:108
  86.7 2.1 fusion.14
  91.4 19.7 %all-gather = f32[128,128]{1,0:T(8,128)S(1)} all-gather(f32[16,128]{1,0:T(8,128)S(1)} %get-tuple-element.266), channel_id=2, replica_groups=mesh['pos'=8,'ch'=32] {'pos'}, dimensions={0}, use_global_device_ids=true | all-gather | bytes 73728 | tf_op jit(solution)/shard_map/all_gather | solution.py:16
  111.1 18.2 %all-gather.2 = f32[128,128]{1,0:T(8,128)S(1)} all-gather(f32[16,128]{1,0:T(8,128)S(1)} %get-tuple-element.253), channel_id=4, replica_groups=mesh['pos'=8,'ch'=32] {'pos'}, dimensions={0}, use_global_device_ids=true | all-gather | bytes 73728 | tf_op jit(solution)/shard_map/all_gather | solution.py:16
  129.8 2.5 fusion.11
  133.8 18.2 %all-gather.1 = f32[128,128]{1,0:T(8,128)S(1)} all-gather(f32[16,128]{1,0:T(8,128)S(1)} %get-tuple-element.221), channel_id=3, replica_groups=mesh['pos'=8,'ch'=32] {'pos'}, dimensions={0}, use_global_device_ids=true | all-gather | bytes 73728 | tf_op jit(solution)/shard_map/all_gather | solution.py:16
  153.5 16.1 %select_bitcast_fusion.1 = f32[128,128,128]{1,0,2:T(8,128)} fusion(pred[128,128]{1,0:T(8,128)(4,1)} %get-tuple-element.268, f32[8,128,128]{1,0,2:T(8,128)S(1)} %copy.288, f32[8,128,128]{1,0,2:T(8,128)S(1)} %copy.297), kind=kOutput, calls=%fused_computation.7 | convolution fusion | flops 203423744 | bytes 9453568 | tf_op jit(solution)/shard_map/transpose(jvp(dts,nsd->ntd))/dot_general | solution.py:49
  169.6 9.4 %copy.324 = f32[128,128,128]{2,1,0:T(8,128)} copy(f32[128,128,128]{1,0,2:T(8,128)} %select_bitcast_fusion.1) | data formatting | bytes 16777216 | tf_op jit(solution)/shard_map/transpose(jvp(jit(_where)))/select_n | solution.py:46
  179.0 98.3 %scatter_custom_fusion = f32[128,128]{0,1:T(8,128)S(1)} fusion(s32[16384]{0:T(1024)} %fusion.47, f32[16384,128]{1,0:T(8,128)} %bitcast.435, f32[]{:T(128)} %constant.84.clone.1), kind=kCustom, calls=%fused_computation.89 | custom fusion | flops 2097152 | bytes 66048 | tf_op jit(solution)/shard_map/transpose(jvp(jit(_take)))/scatter-add | solution.py:47
  278.1 2.4 fusion.16
  280.5 4.9 fusion.10
  288.9 55.2 %gather_fusion = f32[16384,128]{1,0:T(8,128)} fusion(f32[128,128]{0,1:T(8,128)S(1)} %copy.320, s32[16384]{0:T(1024)S(1)} %broadcast_clamp_fusion), kind=kCustom, calls=%fused_computation | custom fusion | bytes 16842752 | tf_op jit(solution)/shard_map/jvp(jit(_take))/gather | solution.py:47
  344.1 7.7 %select_bitcast_fusion = f32[128,128,128]{0,2,1:T(8,128)} fusion(f32[128,128,128]{2,1,0:T(8,128)} %bitcast.434, pred[128,128]{1,0:T(8,128)(4,1)S(1)} %copy-done.16, pred[128,128]{1,0:T(8,128)(4,1)S(1)} %copy-done.30), kind=kLoop, calls=%fused_computation.6 | loop fusion | flops 4194304 | bytes 16809984 | tf_op jit(solution)/shard_map/jvp(jit(_where))/select_n | solution.py:46
  351.7 9.3 %copy.289 = f32[128,128,128]{2,1,0:T(8,128)} copy(f32[128,128,128]{0,2,1:T(8,128)} %select_bitcast_fusion) | data formatting | bytes 16777216 | tf_op jit(solution)/shard_map/jvp(jit(_where))/select_n | solution.py:46
  361.1 16.1 %fusion.4 = f32[8,128,128]{1,0,2:T(8,128)} fusion(f32[128,8,128]{2,1,0:T(8,128)S(1)} %fusion.16, f32[8,128,128]{1,0,2:T(8,128)S(1)} %copy.288, f32[128,128,128]{2,1,0:T(8,128)} %copy.289), kind=kOutput, calls=%fused_computation.17 | convolution fusion | flops 201457664 | bytes 9961472 | tf_op jit(solution)/shard_map/jvp(dts,nsd->ntd)/dot_general | solution.py:49
  377.2 2.1 copy.323
  380.9 2.0 copy.300
  382.9 2.4 fusion.7
  385.3 9.6 %fusion.6 = f32[8,128,128]{1,0,2:T(8,128)S(1)} fusion(f32[8,128,128]{1,0,2:T(8,128)S(1)} %fusion.7, f32[128,128,128]{2,1,0:T(8,128)} %copy.289, f32[8,128,128]{1,0,2:T(8,128)S(1)} %copy.297), kind=kOutput, calls=%fused_computation.21 | convolution fusion | flops 201457664 | bytes 9961472 | tf_op jit(solution)/shard_map/transpose(jvp(dts,nsd->ntd))/dot_general | solution.py:49
  394.9 2.1 fusion.5
  398.2 2.3 fusion.20
  400.5 5.6 convolution_convert_fusion
  406.2 5.5 convert_bitcast_fusion
  411.8 12.0 %copy.325 = bf16[4096,1024]{1,0:T(8,128)(2,1)} copy(bf16[4096,1024]{0,1:T(8,128)(2,1)} %convert_bitcast_fusion) | data formatting | bytes 16777216
  424.7 2.4 fusion.3
  427.1 2.3 fusion.2
  429.7 1.8 fusion.12
  431.6 24.5 %all-reduce.7 = (bf16[128,16]{1,0:T(8,128)(2,1)S(1)}, bf16[128,16]{0,1:T(8,128)(2,1)S(1)}, bf16[128]{0:T(256)(128)(2,1)S(1)}) all-reduce(bf16[128,16]{1,0:T(8,128)(2,1)S(1)} %add_convert_fusion, bf16[128,16]{0,1:T(8,128)(2,1)S(1)} %fusion.71, bf16[128]{0:T(256)(128)(2,1)S(1)} %copy-done.36), channel_id=1, replica_groups=mesh['pos'=8,'ch'=32] {'pos'}, use_global_device_ids=true, to_apply=%region_10.11 | all-reduce | flops 4224 | bytes 16896 | tf_op jit(solution)/shard_map/psum | solution.py:132
  457.9 37.1 %all-reduce.10.cloned.1.call-done = bf16[128,4096]{1,0:T(8,128)(2,1)} async-done(((bf16[128,4096]{1,0:T(8,128)(2,1)}), bf16[128,4096]{1,0:T(8,128)(2,1)}) %all-reduce.10.cloned.1.call-update) | async-done | bytes 1048592 | tf_op jit(solution)/shard_map/psum | solution.py:135
  495.0 2.8 convert_element_type.105
  497.8 102.4 %reduce-scatter.4.cloned.1.call-done = bf16[128,1024]{1,0:T(8,128)(2,1)} async-done(((bf16[4096,1024]{1,0:T(8,128)(2,1)}), bf16[128,1024]{1,0:T(8,128)(2,1)}) %reduce-scatter.4.cloned.1.call-update) | async-done | bytes 262160
  (152 shorter events, 25.7 us)
Async XLA Ops:
  7.2 72.1 %copy-start = (bf16[128,4096]{1,0:T(8,128)(2,1)S(1)}, bf16[128,4096]{1,0:T(8,128)(2,1)}, u32[]{:S(2)}) copy-start(bf16[128,4096]{1,0:T(8,128)(2,1)} %param.19) | copy-start | bytes 3145732
  7.2 72.1 %all-gather.5.cloned.1.call-start = ((), (), s32[]{:S(2)}) async-start(), calls=%async_computation.1 | async-start | bytes 8650752 | tf_op jit(solution)/shard_map/all_gather | solution.py:106
  7.9 487.1 %all-reduce.10.cloned.1.call-start = ((), (), s32[]{:S(2)}) async-start(), calls=%async_computation.2 | async-start | bytes 2097152 | tf_op jit(solution)/shard_map/psum | solution.py:135
  8.8 271.7 %copy-start.9 = (f32[128,16]{1,0:T(8,128)}, f32[128,16]{1,0:T(8,128)S(1)}, u32[]{:S(2)}) copy-start(f32[128,16]{1,0:T(8,128)S(1)} %copy.287) | copy-start | bytes 24580
  9.6 79.3 %copy-start.25 = (f32[128,16]{1,0:T(8,128)}, f32[128,16]{1,0:T(8,128)S(1)}, u32[]{:S(2)}) copy-start(f32[128,16]{1,0:T(8,128)S(1)} %copy.328) | copy-start | bytes 24580
  13.2 73.5 %copy-start.41 = (f32[128]{0:T(128)}, f32[128]{0:T(128)S(1)}, u32[]{:S(2)}) copy-start(f32[128]{0:T(128)S(1)} %iota_convert_fusion) | copy-start | bytes 1540
  15.6 73.3 %copy-start.4 = (f32[128,16]{0,1:T(8,128)S(1)}, f32[128,16]{0,1:T(8,128)}, u32[]{:S(2)}) copy-start(f32[128,16]{0,1:T(8,128)} %param.17) | copy-start | bytes 24580
  88.9 40.9 %copy-start.7 = (f32[128,8,16]{0,2,1:T(8,128)}, f32[128,8,16]{0,2,1:T(8,128)S(1)}, u32[]{:S(2)}) copy-start(f32[128,8,16]{0,2,1:T(8,128)S(1)} %copy.298) | copy-start | bytes 196612
  89.6 89.4 %copy-start.17 = (f32[16,128]{1,0:T(8,128)}, f32[16,128]{1,0:T(8,128)S(1)}, u32[]{:S(2)}) copy-start(f32[16,128]{1,0:T(8,128)S(1)} %get-tuple-element.248) | copy-start | bytes 24580
  90.8 88.2 %copy-start.19 = (f32[16,128]{1,0:T(8,128)}, f32[16,128]{1,0:T(8,128)S(1)}, u32[]{:S(2)}) copy-start(f32[16,128]{1,0:T(8,128)S(1)} %get-tuple-element.250) | copy-start | bytes 24580
  129.5 155.8 %copy-start.5 = (f32[16,128]{1,0:T(8,128)}, f32[16,128]{1,0:T(8,128)S(1)}, u32[]{:S(2)}) copy-start(f32[16,128]{1,0:T(8,128)S(1)} %get-tuple-element.137) | copy-start | bytes 24580
  152.3 26.7 %copy-start.14 = (f32[16,128]{1,0:T(8,128)}, f32[16,128]{1,0:T(8,128)S(1)}, u32[]{:S(2)}) copy-start(f32[16,128]{1,0:T(8,128)S(1)} %get-tuple-element.252) | copy-start | bytes 24580
  169.5 108.5 %copy-start.42 = (f32[128]{0:T(128)S(1)}, f32[128]{0:T(128)}, u32[]{:S(2)}) copy-start(f32[128]{0:T(128)} %copy-done.41) | copy-start | bytes 1540
  169.5 116.6 %copy-start.21 = (f32[16,128]{1,0:T(8,128)S(1)}, f32[16,128]{1,0:T(8,128)}, u32[]{:S(2)}) copy-start(f32[16,128]{1,0:T(8,128)} %get-tuple-element.254) | copy-start | bytes 24580
  169.5 116.6 %copy-start.32 = (f32[1,16,128]{2,1,0:T(8,128)S(1)}, f32[1,16,128]{2,1,0:T(8,128)}, u32[]{:S(2)}) copy-start(f32[1,16,128]{2,1,0:T(8,128)} %get-tuple-element.247) | copy-start | bytes 24580
  169.5 116.6 %copy-start.33 = (f32[1,16,128]{2,1,0:T(8,128)S(1)}, f32[1,16,128]{2,1,0:T(8,128)}, u32[]{:S(2)}) copy-start(f32[1,16,128]{2,1,0:T(8,128)} %get-tuple-element.249) | copy-start | bytes 24580
  169.5 116.6 %copy-start.34 = (f32[1,16,128]{2,1,0:T(8,128)S(1)}, f32[1,16,128]{2,1,0:T(8,128)}, u32[]{:S(2)}) copy-start(f32[1,16,128]{2,1,0:T(8,128)} %get-tuple-element.262) | copy-start | bytes 24580
  169.6 116.6 %copy-start.35 = (f32[1,16,128]{2,1,0:T(8,128)S(1)}, f32[1,16,128]{2,1,0:T(8,128)}, u32[]{:S(2)}) copy-start(f32[1,16,128]{2,1,0:T(8,128)} %unstack.64) | copy-start | bytes 24580
  277.3 66.8 %copy-start.12 = (f32[128,128]{0,1:T(8,128)}, f32[128,128]{0,1:T(8,128)S(1)}, u32[]{:S(2)}) copy-start(f32[128,128]{0,1:T(8,128)S(1)} %scatter_custom_fusion) | copy-start | bytes 196612
  288.9 55.2 %copy-start.16 = (pred[128,128]{1,0:T(8,128)(4,1)S(1)}, pred[128,128]{1,0:T(8,128)(4,1)}, u32[]{:S(2)}) copy-start(pred[128,128]{1,0:T(8,128)(4,1)} %get-tuple-element.268) | copy-start | bytes 49156
  288.9 55.2 %copy-start.30 = (pred[128,128]{1,0:T(8,128)(4,1)S(1)}, pred[128,128]{1,0:T(8,128)(4,1)}, u32[]{:S(2)}) copy-start(pred[128,128]{1,0:T(8,128)(4,1)} %get-tuple-element.269) | copy-start | bytes 49156
  361.1 21.8 %copy-start.10 = (f32[128,16]{1,0:T(8,128)S(1)}, f32[128,16]{1,0:T(8,128)}, u32[]{:S(2)}) copy-start(f32[128,16]{1,0:T(8,128)} %copy-done.9) | copy-start | bytes 24580
  377.2 21.0 %copy-start.1 = (f32[1024,128]{1,0:T(8,128)S(1)}, f32[1024,128]{1,0:T(8,128)}, u32[]{:S(2)}) copy-start(f32[1024,128]{1,0:T(8,128)} %get-tuple-element.267) | copy-start | bytes 1572868
  377.2 21.0 %copy-start.3 = (bf16[1024,128]{1,0:T(8,128)(2,1)S(1)}, bf16[1024,128]{1,0:T(8,128)(2,1)}, u32[]{:S(2)}) copy-start(bf16[1024,128]{1,0:T(8,128)(2,1)} %param.14) | copy-start | bytes 786436
  382.9 12.0 %copy-start.23 = (f32[128,16]{1,0:T(8,128)S(1)}, f32[128,16]{1,0:T(8,128)}, u32[]{:S(2)}) copy-start(f32[128,16]{1,0:T(8,128)} %copy.303) | copy-start | bytes 24580
  382.9 12.0 %copy-start.27 = (f32[128,16]{1,0:T(8,128)S(1)}, f32[128,16]{1,0:T(8,128)}, u32[]{:S(2)}) copy-start(f32[128,16]{1,0:T(8,128)} %copy.302) | copy-start | bytes 24580
  382.9 12.0 %copy-start.37 = (f32[128]{0:T(128)S(1)}, f32[128]{0:T(128)}, u32[]{:S(2)}) copy-start(f32[128]{0:T(128)} %broadcast_subtract_fusion) | copy-start | bytes 1540
  382.9 12.0 %copy-start.39 = (f32[8]{0:T(128)S(1)}, f32[8]{0:T(128)}, u32[]{:S(2)}) copy-start(f32[8]{0:T(128)} %convert_subtract_fusion) | copy-start | bytes 100
  406.2 194.0 %reduce-scatter.4.cloned.1.call-start = ((), (), s32[]{:S(2)}) async-start(), calls=%async_computation.3 | async-start | bytes 8650752
  423.9 5.8 copy-start.43
  423.9 7.6 %copy-start.29 = (f32[128,16]{1,0:T(8,128)S(1)}, f32[128,16]{1,0:T(8,128)}, u32[]{:S(2)}) copy-start(f32[128,16]{1,0:T(8,128)} %get-tuple-element.218) | copy-start | bytes 24580
  423.9 7.7 %copy-start.36 = (bf16[128]{0:T(256)(128)(2,1)S(1)}, bf16[128]{0:T(256)(128)(2,1)}, u32[]{:S(2)}) copy-start(bf16[128]{0:T(256)(128)(2,1)} %get-tuple-element.245) | copy-start | bytes 772
  (15 other events, 54.9 us)
Sparse Core Ops, SparseCore 0:
  10.5 68.7 all-gather.4
  406.3 88.6 all-reduce.9
  499.1 101.0 reduce-scatter.3
where the time goes:
time: 616 us; the launch traced here: 609 us
  waiting for transfers between devices  204 us (33%)
  other arithmetic  123 us (20%)
  local copies, waits for them, and re-layouts  103 us (17%)
  matrix products  82.9 us (13%)
  blocking collectives  80.6 us (13%)
  between operations  15.2 us (2%)
    unnamed x4, waiting for transfers between devices  103 us
    scatter-add x1, other arithmetic, device_output(): jnp.take(kernel, jnp.clip(lag_grid, 0, SUB - 1), axis=1)  98.3 us
    all_gather x1, waiting for transfers between devices, shards(): shard_piece = lax.all_gather(d_out, 'ch', axis=1, tiled=True)  63.6 us
    all_gather x3, blocking collectives, carried_in(): gathered = jax.tree.map(lambda a: lax.all_gather(a, axis), part)  56.1 us
    gather x1, local copies, waits for them, and re-layouts, device_output(): jnp.take(kernel, jnp.clip(lag_grid, 0, SUB - 1), axis=1)  55.2 us
    dot_general x3, matrix products, device_output(): intra_part = jnp.einsum('dts,nsd->ntd', toeplitz, blocks, precision=highest)  41.8 us
    psum x1, waiting for transfers between devices, shards(): lax.psum(d_weight.astype(jnp.bfloat16), 'pos').astype(jnp.float32)  37.1 us
    psum x1, blocking collectives, shards(): lax.psum(d_residue.astype(jnp.bfloat16), 'pos').astype(jnp.float32)  24.5 us
  transfers between devices with their start and end apart: 3, of which 3 were waited for; matrix products, arithmetic and copies ran while one was open for 6% of the time, Pallas kernels for 0%

commit v1 on v0

v1 whole, which is shorter than its diff:
```python
import functools

import jax
import jax.numpy as jnp
from jax import lax
from jax.experimental import pallas as pl
from jax.experimental.pallas import tpu as pltpu
from jax.sharding import PartitionSpec as P

f32 = jnp.float32
bf16 = jnp.bfloat16
MODES = 16
GROUP = 8
NSUB = 8
UNROLL = 4


def rows_of(s):
    return pl.ds(pl.multiple_of(s * NSUB, NSUB), NSUB)


def interleave(dst, val):
    sub = val.shape[0] // NSUB
    for n in range(NSUB):
        dst[pl.ds(n, sub, stride=NSUB), :] = val[n * sub : (n + 1) * sub]


def deinterleave(src):
    sub = src.shape[0] // NSUB
    return jnp.concatenate([src[pl.ds(n, sub, stride=NSUB), :] for n in range(NSUB)], axis=0)


def spread(a):
    return jnp.broadcast_to(a[:, None, :], (a.shape[0], NSUB, a.shape[1]))


def place_of(shape):
    return lax.broadcasted_iota(jnp.int32, shape, 1)


def scan_states(src, rate, reverse):
    sub = src.shape[0] // NSUB
    lam = spread(jnp.exp(-rate))

    def step(i, h):
        s = sub - 1 - i if reverse else i
        return lam * h + src[rows_of(s), :][None]

    p = lax.fori_loop(0, sub, step, jnp.zeros_like(lam), unroll=UNROLL)
    place = place_of(p.shape)
    for k in (1, 2, 4):
        moved = pltpu.roll(p, NSUB - k if reverse else k, 1)
        ok = place < NSUB - k if reverse else place >= k
        p = p + spread(jnp.exp(-rate * (sub * k))) * jnp.where(ok, moved, 0.0)
    return p


def edge_of(p, reverse):
    return jnp.sum(jnp.where(place_of(p.shape) == (0 if reverse else NSUB - 1), p, 0.0), axis=1)


def entering_of(p, rate, sub, carry, reverse):
    place = place_of(p.shape)
    moved = pltpu.roll(p, NSUB - 1 if reverse else 1, 1)
    ok = place < NSUB - 1 if reverse else place >= 1
    steps = (NSUB - 1 - place if reverse else place).astype(f32) * float(sub)
    return jnp.where(ok, moved, 0.0) + jnp.exp(-spread(rate) * steps) * spread(carry)


def forward_pass(xs, ys, hs, rate, residue, start):
    sub = xs.shape[0] // NSUB
    for lo in range(0, MODES, GROUP):
        part = slice(lo, lo + GROUP)
        lam, res = spread(jnp.exp(-rate[part])), spread(residue[part])

        def step(s, h):
            if hs is not None:
                hs[s, part] = h
            h = lam * h + xs[rows_of(s), :][None]
            if ys is not None:
                y = jnp.sum(res * h, axis=0)
                ys[rows_of(s), :] = y if lo == 0 else ys[rows_of(s), :] + y
            return h

        lax.fori_loop(0, sub, step, start[part], unroll=UNROLL)


def backward_pass(xs, gs, ms, hs, rate, residue, start):
    sub = xs.shape[0] // NSUB
    d_res, d_rate = [], []
    for lo in range(0, MODES, GROUP):
        part = slice(lo, lo + GROUP)
        lam, res = spread(jnp.exp(-rate[part])), spread(residue[part])

        def step(i, carry):
            a, dr, dt = carry
            s = sub - 1 - i
            a = lam * a + gs[rows_of(s), :][None]
            m = jnp.sum(res * a, axis=0)
            ms[rows_of(s), :] = m if lo == 0 else ms[rows_of(s), :] + m
            return a, dr + a * xs[rows_of(s), :][None], dt + a * hs[s, part]

        zero = jnp.zeros_like(lam)
        _, dr, dt = lax.fori_loop(0, sub, step, (start[part], zero, zero), unroll=UNROLL)
        d_res.append(jnp.sum(dr, axis=1))
        d_rate.append(-residue[part] * jnp.exp(-rate[part]) * jnp.sum(dt, axis=1))
    return jnp.concatenate(d_res, axis=0), jnp.concatenate(d_rate, axis=0)


def k_sum(k, v, rate, s_out, xs):
    interleave(xs, k[...].astype(f32) * v[...].astype(f32))
    s_out[...] = edge_of(scan_states(xs, rate[...], False), False)


def k_main(q, k, v, rate, residue, skip, carry, field, product, xs, ys):
    x = k[...].astype(f32) * v[...].astype(f32)
    interleave(xs, x)
    sub = xs.shape[0] // NSUB
    p = scan_states(xs, rate[...], False)
    start = entering_of(p, rate[...], sub, carry[...], False)
    forward_pass(xs, ys, None, rate[...], residue[...], start)
    c = deinterleave(ys) + skip[...] * x
    field[...] = c
    product[...] = (q[...].astype(f32) * c).astype(bf16)


def k_back_sum(q, dp, rate, a_out, gs):
    interleave(gs, dp[...] * q[...].astype(f32))
    a_out[...] = edge_of(scan_states(gs, rate[...], True), True)


def k_back(q, k, v, dp, field, rate, residue, skip, carry, later, dq, dk, dv, dres, drate, dskip, xs, gs, ms, hs):
    kk, vv = k[...].astype(f32), v[...].astype(f32)
    x = kk * vv
    g = dp[...] * q[...].astype(f32)
    interleave(xs, x)
    interleave(gs, g)
    sub = xs.shape[0] // NSUB
    r = rate[...]
    start = entering_of(scan_states(xs, r, False), r, sub, carry[...], False)
    forward_pass(xs, None, hs, r, residue[...], start)
    start = entering_of(scan_states(gs, r, True), r, sub, later[...], True)
    dres[...], drate[...] = backward_pass(xs, gs, ms, hs, r, residue[...], start)
    dskip[...] = jnp.sum(x * g, axis=0, keepdims=True)
    dq[...] = (dp[...] * field[...]).astype(bf16)
    dm = deinterleave(ms) + skip[...] * g
    dk[...] = (dm * vv).astype(bf16)
    dv[...] = (dm * kk).astype(bf16)


def call(kernel, outs, scratch, *args):
    return pl.pallas_call(
        kernel,
        out_shape=outs,
        scratch_shapes=scratch,
        compiler_params=pltpu.CompilerParams(vmem_limit_bytes=48 * 1024 * 1024),
    )(*args)


def carried(edge, rate, steps, weights, reverse):
    every = lax.all_gather(edge, "pos")
    place = lax.axis_index("pos")
    total = jnp.zeros_like(edge)
    for k in (1, 2, 3):
        other = (place + k if reverse else place - k) % every.shape[0]
        total += weights[k - 1] * jnp.exp(-rate * (steps * (k - 1))) * every[other]
    return total


def shards(queries, keys, values, residue, rate, skip, w_out, lengths, d_out):
    t, c = queries.shape
    rate, residue, skip = rate.T, residue.T, skip[None, :]
    place, count = lax.axis_index("pos"), lax.axis_size("pos")
    ends = jnp.cumsum(lengths)
    document = lambda b: jnp.sum((ends <= b).astype(jnp.int32))

    def weight(other):
        inside = (other >= 0) & (other < count)
        return jnp.where(inside & (document(other) == document(place)), 1.0, 0.0).astype(f32)

    before = [weight(place - k) for k in (1, 2, 3)]
    after = [weight(place + k) for k in (1, 2, 3)]
    state = jax.ShapeDtypeStruct((MODES, c), f32)
    wide = jax.ShapeDtypeStruct((t, c), f32)
    thin = jax.ShapeDtypeStruct((t, c), bf16)
    big = pltpu.VMEM((t, c), f32)
    edge = call(k_sum, state, [big], keys, values, rate)
    carry = carried(edge, rate, float(t), before, False)
    field, product = call(
        k_main, (wide, thin), [big, big], queries, keys, values, rate, residue, skip, carry
    )
    gathered = lax.all_gather(d_out, "ch", axis=1, tiled=True)
    dp = lax.dot_general(gathered, w_out, (((1,), (1,)), ((), ())), preferred_element_type=f32)
    edge = call(k_back_sum, state, [big], queries, dp, rate)
    later = carried(edge, rate, float(t), after, True)
    dq, dk, dv, dres, drate, dskip = call(
        k_back,
        (thin, thin, thin, state, state, jax.ShapeDtypeStruct((1, c), f32)),
        [big, big, big, pltpu.VMEM((t // NSUB, MODES, NSUB, c), f32)],
        queries, keys, values, dp, field, rate, residue, skip, carry, later,
    )
    dw = lax.dot_general(product, gathered, (((0,), (0,)), ((), ())), preferred_element_type=f32)
    dw = lax.psum(dw.astype(bf16), "pos").astype(f32)
    part = lax.dot_general(w_out, product, (((0,), (1,)), ((), ())), preferred_element_type=f32)
    out = lax.psum_scatter(part.astype(bf16), "ch", scatter_dimension=0, tiled=True).T
    small = lax.psum(jnp.concatenate([dres, drate, dskip], axis=0).astype(bf16), "pos").astype(f32)
    return out, dq, dk, dv, small[:MODES].T, small[MODES : 2 * MODES].T, small[2 * MODES], dw


def solution(mesh):
    both, chan = P("pos", "ch"), P("ch", None)
    return jax.shard_map(
        shards,
        mesh=mesh,
        in_specs=(both, both, both, chan, chan, P("ch"), chan, P(), both),
        out_specs=(both, both, both, both, chan, chan, P("ch"), chan),
        check_vma=False,
    )
```

time: 616 us -> 302 us (0.49)
  other arithmetic: 123 us -> 4.36 us
  local copies, waits for them, and re-layouts: 103 us -> 17.5 us
  matrix products: 82.9 us -> 13.7 us
  waiting for transfers between devices: 204 us -> 167 us
  blocking collectives: 80.6 us -> 65.3 us
  Pallas kernels: 0 us -> 10.8 us
  between operations: 15.2 us -> 21.9 us
    scatter-add x1 -> x0, other arithmetic: 98.3 us -> none  [device_output(): jnp.take(kernel, jnp.clip(lag_grid, 0, SUB - 1), axis=1)]
    dot_general x15 -> x3, matrix products: 82.9 us -> 13.7 us  [the longest x1 5.86 us: shards(): lax.dot_general(gathered, w_out, (((1,), (1,)), ((), ())), preferred_elem...]
    gather x1 -> x0, local copies, waits for them, and re-layouts: 55.2 us -> none  [device_output(): jnp.take(kernel, jnp.clip(lag_grid, 0, SUB - 1), axis=1)]
    all_gather x1, waiting for transfers between devices: 63.6 us -> 35.2 us  [shards(): gathered = lax.all_gather(d_out, 'ch', axis=1, tiled=True)]
    select_n x2 -> x0, local copies, waits for them, and re-layouts: 18.7 us -> none  [device_output(): jnp.where(lag_grid[None] >= 0, jnp.take(kernel, jnp.clip(lag_grid, 0, SUB...]
    all_gather x3 -> x2, blocking collectives: 56.1 us -> 42.8 us  [carried(): every = lax.all_gather(edge, 'pos')]
    pallas_call x0 -> x4, Pallas kernels: none -> 10.8 us  [call(): pl.pallas_call(kernel, out_shape=outs, scratch_shapes=scratch, compiler_p...]
    psum x1, waiting for transfers between devices: 37.1 us -> 28.5 us  [shards(): dw = lax.psum(dw.astype(bf16), 'pos').astype(f32)]
  transfers between devices with their start and end apart: 3 -> 3, of which waited for: 3 -> 3; matrix products, arithmetic and copies ran while one was open for 6% -> 8% of each run, Pallas kernels for 0% -> 2%
where the time goes in v1:
time: 302 us; the launch traced here: 300 us
  waiting for transfers between devices  167 us (55%)
  blocking collectives  65.3 us (22%)
  between operations  21.9 us (7%)
  local copies, waits for them, and re-layouts  17.5 us (6%)
  matrix products  13.7 us (5%)
  Pallas kernels  10.8 us (4%)
  other arithmetic  4.36 us (1%)
    unnamed x4, waiting for transfers between devices  103 us
    all_gather x2, blocking collectives, carried(): every = lax.all_gather(edge, 'pos')  42.8 us
    all_gather x1, waiting for transfers between devices, shards(): gathered = lax.all_gather(d_out, 'ch', axis=1, tiled=True)  35.2 us
    psum x1, waiting for transfers between devices, shards(): dw = lax.psum(dw.astype(bf16), 'pos').astype(f32)  28.5 us
    psum x1, blocking collectives, shards(): lax.psum(jnp.concatenate([dres, drate, dskip], axis=0).astype(bf16), 'pos')  22.6 us
    unnamed x24, local copies, waits for them, and re-layouts  16.4 us
    pallas_call x4, Pallas kernels, call(): pl.pallas_call(kernel, out_shape=outs, scratch_shapes=scratch, compiler_p...  10.8 us
  transfers between devices with their start and end apart: 3, of which 3 were waited for; matrix products, arithmetic and copies ran while one was open for 8% of the time, Pallas kernels for 2%

profile of v1, /device:TPU:1, one launch (start us, length us, event | category | flops | bytes accessed | tf_op | source)
XLA Modules:
  0.0 300.5 jit_solution(6287494739081798408)
XLA Ops:
  7.2 0.0 copy-start
  7.2 0.0 copy-start.3
  7.2 0.0 copy-start.7
  7.2 0.0 all-gather.4.cloned.1.call-start
  7.3 0.7 all-gather.4.cloned.1.call-update
  8.0 0.0 all-reduce.2.cloned.1.call-start
  8.1 0.8 reduce-window.9
  9.0 0.7 fusion.8
  17.6 0.9 copy-done.2
  18.5 0.9 copy-done.4
  19.5 0.7 copy-done.6
  20.2 0.9 shard_map.152
  21.1 23.1 %all-gather = f32[128,128]{1,0:T(8,128)S(1)} all-gather(f32[16,128]{1,0:T(8,128)S(1)} %shard_map.152), channel_id=2, replica_groups=mesh['pos'=8,'ch'=32] {'pos'}, dimensions={0}, use_global_device_ids=true | all-gather | bytes 73728 | tf_op jit(solution)/shard_map/all_gather | solution.py:161
  44.1 35.2 %all-gather.4.cloned.1.call-done = bf16[1024,4096]{1,0:T(8,128)(2,1)} async-done(((bf16[1024,128]{1,0:T(8,128)(2,1)}), bf16[1024,4096]{1,0:T(8,128)(2,1)}) %all-gather.4.cloned.1.call-update) | async-done | bytes 8388624 | tf_op jit(solution)/shard_map/all_gather | solution.py:192
  79.3 5.9 %fusion.11.dp = f32[1024,128]{1,0:T(8,128)S(1)} fusion(bf16[1024,4096]{1,0:T(8,128)(2,1)} %all-gather.4.cloned.1.call-done, bf16[128,4096]{1,0:T(8,128)(2,1)S(1)} %copy-done), kind=kOutput, calls=%fused_computation.33 | convolution fusion | flops 1073741824 | bytes 9961472 | tf_op jit(solution)/shard_map/dot_general | solution.py:193
  85.2 0.9 shard_map.154
  86.1 19.7 %all-gather.1 = f32[128,128]{1,0:T(8,128)S(1)} all-gather(f32[16,128]{1,0:T(8,128)S(1)} %shard_map.154), channel_id=3, replica_groups=mesh['pos'=8,'ch'=32] {'pos'}, dimensions={0}, use_global_device_ids=true | all-gather | bytes 73728 | tf_op jit(solution)/shard_map/all_gather | solution.py:161
  105.9 2.7 shard_map.153
  108.6 2.3 convolution_convert_fusion
  110.8 0.0 all-reduce.2.cloned.1.call-update
  110.8 0.0 reduce-scatter.4.cloned.1.call-start
  110.9 5.5 %convert_bitcast_fusion = bf16[4096,1024]{0,1:T(8,128)(2,1)} fusion(bf16[1024,128]{1,0:T(8,128)(2,1)S(1)} %get-tuple-element.16, bf16[128,4096]{1,0:T(8,128)(2,1)S(1)} %copy-done), kind=kOutput, calls=%fused_computation | convolution fusion | flops 1077936128 | bytes 9699328 | tf_op jit(solution)/shard_map/dot_general | solution.py:204
  116.4 12.0 %copy.17 = bf16[4096,1024]{1,0:T(8,128)(2,1)} copy(bf16[4096,1024]{0,1:T(8,128)(2,1)} %convert_bitcast_fusion) | data formatting | bytes 16777216
  128.4 0.0 reduce-scatter.4.cloned.1.call-update
  128.4 6.4 %shard_map.155 = (bf16[1024,128]{1,0:T(8,128)(2,1)}, bf16[1024,128]{1,0:T(8,128)(2,1)}, bf16[1024,128]{1,0:T(8,128)(2,1)}, f32[16,128]{1,0:T(8,128)S(1)}, f32[16,128]{1,0:T(8,128)S(1)}, /*index=5*/f32[1,128]{1,0:T(1,128)S(1)}) custom-call(bf16[1024,128]{1,0:T(8,128)(2,1)S(1)} %copy-done.1, bf16[1024,128]{1,0:T(8,128)(2,1)S(1)} %copy-done.3, ...), custom_call_target="tpu_custom_call" | custom-call | tf_op jit(solution)/shard_map/pallas_call | solution.py:152
  134.9 22.6 %psum.14 = bf16[33,128]{1,0:T(8,128)(2,1)S(1)} all-reduce(bf16[33,128]{1,0:T(8,128)(2,1)S(1)} %pad_maximum_fusion), channel_id=1, replica_groups=mesh['pos'=8,'ch'=32] {'pos'}, use_global_device_ids=true, to_apply=%region_9.10 | all-reduce | flops 4224 | bytes 16896 | tf_op jit(solution)/shard_map/psum | solution.py:206
  157.5 0.5 slice_bitcast_fusion.2
  158.0 0.6 slice_bitcast_fusion
  158.6 28.5 %all-reduce.2.cloned.1.call-done = bf16[128,4096]{1,0:T(8,128)(2,1)} async-done(((bf16[128,4096]{1,0:T(8,128)(2,1)}), bf16[128,4096]{1,0:T(8,128)(2,1)}) %all-reduce.2.cloned.1.call-update) | async-done | bytes 1048592 | tf_op jit(solution)/shard_map/psum | solution.py:203
  187.0 2.8 convert_element_type.60
  189.8 102.4 %reduce-scatter.4.cloned.1.call-done = bf16[128,1024]{1,0:T(8,128)(2,1)} async-done(((bf16[4096,1024]{1,0:T(8,128)(2,1)}), bf16[128,1024]{1,0:T(8,128)(2,1)}) %reduce-scatter.4.cloned.1.call-update) | async-done | bytes 262160
  292.2 1.8 copy.18
  (22 shorter events, 0.1 us)
Async XLA Ops:
  7.2 72.2 %copy-start = (bf16[128,4096]{1,0:T(8,128)(2,1)S(1)}, bf16[128,4096]{1,0:T(8,128)(2,1)}, u32[]{:S(2)}) copy-start(bf16[128,4096]{1,0:T(8,128)(2,1)} %param.15) | copy-start | bytes 3145732
  7.2 98.7 %copy-start.3 = (bf16[1024,128]{1,0:T(8,128)(2,1)S(1)}, bf16[1024,128]{1,0:T(8,128)(2,1)}, u32[]{:S(2)}) copy-start(bf16[1024,128]{1,0:T(8,128)(2,1)} %k.5) | copy-start | bytes 786436
  7.2 78.0 %copy-start.7 = (f32[128,16]{0,1:T(8,128)S(1)}, f32[128,16]{0,1:T(8,128)}, u32[]{:S(2)}) copy-start(f32[128,16]{0,1:T(8,128)} %param.13) | copy-start | bytes 24580
  7.2 78.0 %copy-start.1 = (bf16[1024,128]{1,0:T(8,128)(2,1)S(1)}, bf16[1024,128]{1,0:T(8,128)(2,1)}, u32[]{:S(2)}) copy-start(bf16[1024,128]{1,0:T(8,128)(2,1)} %q.5) | copy-start | bytes 786436
  7.2 98.6 %copy-start.9 = (f32[128]{0:T(128)S(1)}, f32[128]{0:T(128)}, u32[]{:S(2)}) copy-start(f32[128]{0:T(128)} %param.14) | copy-start | bytes 1540
  7.2 98.6 %copy-start.8 = (f32[128,16]{0,1:T(8,128)S(1)}, f32[128,16]{0,1:T(8,128)}, u32[]{:S(2)}) copy-start(f32[128,16]{0,1:T(8,128)} %param.12) | copy-start | bytes 24580
  7.2 72.1 %all-gather.4.cloned.1.call-start = ((), (), s32[]{:S(2)}) async-start(), calls=%async_computation.1 | async-start | bytes 8650752 | tf_op jit(solution)/shard_map/all_gather | solution.py:192
  8.0 179.1 %all-reduce.2.cloned.1.call-start = ((), (), s32[]{:S(2)}) async-start(), calls=%async_computation.2 | async-start | bytes 2097152 | tf_op jit(solution)/shard_map/psum | solution.py:203
  17.6 1.0 copy-start.2
  18.5 0.9 copy-start.4
  19.5 0.7 copy-start.6
  20.2 85.7 %copy-start.5 = (bf16[1024,128]{1,0:T(8,128)(2,1)S(1)}, bf16[1024,128]{1,0:T(8,128)(2,1)}, u32[]{:S(2)}) copy-start(bf16[1024,128]{1,0:T(8,128)(2,1)} %v.5) | copy-start | bytes 786436
  79.3 29.2 %copy-start.10 = (bf16[1024,4096]{1,0:T(8,128)(2,1)S(1)}, bf16[1024,4096]{1,0:T(8,128)(2,1)}, u32[]{:S(2)}) copy-start(bf16[1024,4096]{1,0:T(8,128)(2,1)} %all-gather.4.cloned.1.call-done) | copy-start | bytes 25165828
  110.8 181.3 %reduce-scatter.4.cloned.1.call-start = ((), (), s32[]{:S(2)}) async-start(), calls=%async_computation.3 | async-start | bytes 8650752
Sparse Core Ops, SparseCore 0:
  10.5 68.7 all-gather.3
  111.0 76.0 all-reduce.1
  191.1 101.0 reduce-scatter.3

commit v2 on v1

v2 whole, which is shorter than its diff:
```python
import functools

import jax
import jax.numpy as jnp
from jax import lax
from jax.experimental import pallas as pl
from jax.experimental.pallas import tpu as pltpu
from jax.sharding import PartitionSpec as P

f32 = jnp.float32
bf16 = jnp.bfloat16
MODES = 16
GROUP = 8
NSUB = 8
UNROLL = 4
SIDE = 4
CHIPS = SIDE * SIDE
STREAMS = 4
MESH = pl.DeviceIdType.MESH
MIB = 1024 * 1024


def rows_of(s):
    return pl.ds(pl.multiple_of(s * NSUB, NSUB), NSUB)


def interleave(dst, val):
    sub = val.shape[0] // NSUB
    for n in range(NSUB):
        dst[pl.ds(n, sub, stride=NSUB), :] = val[n * sub : (n + 1) * sub]


def deinterleave(src):
    sub = src.shape[0] // NSUB
    return jnp.concatenate([src[pl.ds(n, sub, stride=NSUB), :] for n in range(NSUB)], axis=0)


def spread(a):
    return jnp.broadcast_to(a[:, None, :], (a.shape[0], NSUB, a.shape[1]))


def place_of(shape):
    return lax.broadcasted_iota(jnp.int32, shape, 1)


def scan_states(src, rate, reverse):
    sub = src.shape[0] // NSUB
    lam = spread(jnp.exp(-rate))

    def step(i, h):
        s = sub - 1 - i if reverse else i
        return lam * h + src[rows_of(s), :][None]

    p = lax.fori_loop(0, sub, step, jnp.zeros_like(lam), unroll=UNROLL)
    place = place_of(p.shape)
    for k in (1, 2, 4):
        moved = pltpu.roll(p, NSUB - k if reverse else k, 1)
        ok = place < NSUB - k if reverse else place >= k
        p = p + spread(jnp.exp(-rate * (sub * k))) * jnp.where(ok, moved, 0.0)
    return p


def edge_of(p, reverse):
    return jnp.sum(jnp.where(place_of(p.shape) == (0 if reverse else NSUB - 1), p, 0.0), axis=1)


def entering_of(p, rate, sub, carry, reverse):
    place = place_of(p.shape)
    moved = pltpu.roll(p, NSUB - 1 if reverse else 1, 1)
    ok = place < NSUB - 1 if reverse else place >= 1
    steps = (NSUB - 1 - place if reverse else place).astype(f32) * float(sub)
    return jnp.where(ok, moved, 0.0) + jnp.exp(-spread(rate) * steps) * spread(carry)


def forward_pass(xs, ys, hs, rate, residue, start):
    sub = xs.shape[0] // NSUB
    for lo in range(0, MODES, GROUP):
        part = slice(lo, lo + GROUP)
        lam, res = spread(jnp.exp(-rate[part])), spread(residue[part])

        def step(s, h):
            hs[s, part] = h
            h = lam * h + xs[rows_of(s), :][None]
            y = jnp.sum(res * h, axis=0)
            ys[rows_of(s), :] = y if lo == 0 else ys[rows_of(s), :] + y
            return h

        lax.fori_loop(0, sub, step, start[part], unroll=UNROLL)


def backward_pieces(xs, gs, ms, hs, rate, residue, start, pieces, result):
    sub = xs.shape[0] // NSUB
    span = sub // pieces
    d_res, d_rate = [], []
    for lo in range(0, MODES, GROUP):
        part = slice(lo, lo + GROUP)
        lam, res = spread(jnp.exp(-rate[part])), spread(residue[part])

        def step(i, carry):
            a, dr, dt = carry
            s = sub - 1 - i
            a = lam * a + gs[rows_of(s), :][None]
            m = jnp.sum(res * a, axis=0)
            ms[rows_of(s), :] = m if lo == 0 else ms[rows_of(s), :] + m
            return a, dr + a * xs[rows_of(s), :][None], dt + a * hs[s, part]

        zero = jnp.zeros_like(lam)
        carry = (start[part], zero, zero)
        for piece in range(pieces):
            carry = lax.fori_loop(piece * span, (piece + 1) * span, step, carry, unroll=UNROLL)
            yield
        d_res.append(jnp.sum(carry[1], axis=1))
        d_rate.append(-residue[part] * jnp.exp(-rate[part]) * jnp.sum(carry[2], axis=1))
    result.extend(d_res + d_rate)


class Links:
    def __init__(self):
        self.sent = []

    def copy(self, src, dst, send, recv, device):
        return pltpu.make_async_remote_copy(
            src_ref=src, dst_ref=dst, send_sem=send, recv_sem=recv,
            device_id=device, device_id_type=MESH,
        )

    def send(self, *args):
        c = self.copy(*args)
        c.start()
        self.sent.append(c)

    def drain(self):
        for c in self.sent:
            c.wait_send()
        self.sent = []


class Gather:
    def __init__(self, links, buf, send, recv, z, x, y, core):
        self.links, self.buf, self.send_sem, self.recv_sem = links, buf, send, recv
        self.z, self.at, self.core = z, (x, y), core

    def axes(self, s):
        return (0, 1, 1 - 2 * (s % 2)) if s < 2 else (1, 0, 1 - 2 * (s % 2))

    def region(self, s, i, j):
        a, b, sign = self.axes(s)
        at = list(self.at)
        at[a] = lax.rem(at[a] - sign * i + SIDE, SIDE)
        at[b] = lax.rem(at[b] - sign * j + SIDE, SIDE)
        chip = at[0] * SIDE + at[1]
        rows = self.buf.shape[0] // STREAMS
        wide = self.buf.shape[1] // CHIPS
        return self.buf.at[pl.ds(s * rows, rows), pl.ds(pl.multiple_of(chip * wide, wide), wide)]

    def device(self, s, second):
        sign = self.axes(s)[2]
        axis = self.axes(s)[1 if second else 0]
        at = list(self.at)
        at[axis] = lax.rem(at[axis] + sign + SIDE, SIDE)
        return (self.z, (at[0] * SIDE + at[1]) * 2 + self.core)

    def copy(self, s, i, j, second):
        here = self.region(s, i, j)
        k = i * SIDE + j
        return (
            here, here, self.send_sem.at[s, k, second],
            self.recv_sem.at[s, k + (1 if second else SIDE)], self.device(s, second),
        )

    def wave(self, k):
        for i in range(min(k, SIDE - 1), -1, -1):
            j = k - i
            if j >= SIDE:
                continue
            for s in range(STREAMS):
                if k > 0:
                    second = 1 if j else 0
                    came = self.copy(s, i - (1 - second), j - second, second)
                    here = self.region(s, i, j)
                    self.links.copy(here, here, came[2], came[3], came[4]).wait_recv()
                if j == 0 and i < SIDE - 1:
                    self.links.send(*self.copy(s, i, j, 0))
                if j < SIDE - 1:
                    self.links.send(*self.copy(s, i, j, 1))


def lanes(i, width):
    return pl.ds(pl.multiple_of(i * width, width), width)


def kernel(
    count, q, key, val, w, d_out, rate_ref, res_ref, skip, weights,
    out, dq, dk, dv, small, dw,
    G, H, W2, WC, xs, gs, ys, hs, field, dp, dp_send, prod, out_send, out_all,
    states, state_got, small_all, dw_own, dw_send, dw_got, ring, dw_all,
    g_send, g_recv, h_send, h_recv, loc, one_s, one_r, a2a_s, a2a_r, wz_s, wz_r,
    st_s, st_r, sm_s, sm_r, rs_s, rs_r, ag_s, ag_r,
):
    z, ch = lax.axis_index("pos"), lax.axis_index("ch")
    core, chip = lax.rem(ch, 2), lax.div(ch, 2)
    x, y = lax.div(chip, SIDE), lax.rem(chip, SIDE)
    mate = (z, chip * 2 + 1 - core)
    other = 1 - core
    t, c = q.shape
    half = t // 2
    wide = 2 * c
    n_out = w.shape[1]

    def along(k):
        return (lax.rem(z + k + count, count), ch)

    def chip_at(k):
        return lax.rem(chip + k, CHIPS)

    barrier = pltpu.get_barrier_semaphore()
    peers = [mate] + [along(k) for k in range(1, count)]
    peers += [(z, chip_at(k) * 2 + core) for k in range(1, CHIPS)]
    for device in peers:
        pl.semaphore_signal(barrier, inc=1, device_id=device, device_id_type=MESH)

    mine, its = lanes(core, half), lanes(other, half)
    own_cols = pl.ds(pl.multiple_of(chip * wide + core * c, c), c)
    mate_cols = pl.ds(pl.multiple_of(chip * wide + other * c, c), c)
    slab = c // count
    own_rows = pl.ds(pl.multiple_of(z * slab, slab), slab)
    slab_rows = pl.ds(pl.multiple_of(core * c + z * slab, slab), slab)
    local = [
        pltpu.make_async_copy(d_out.at[mine], G.at[:, own_cols], loc.at[0]),
        pltpu.make_async_copy(w, W2.at[lanes(core, c)], loc.at[1]),
        pltpu.make_async_copy(
            w.at[own_rows, lanes(chip, wide)], WC.at[chip, slab_rows], loc.at[2]
        ),
    ]
    for copy in local:
        copy.start()
    pl.semaphore_wait(barrier, len(peers))

    links = Links()
    links.send(d_out.at[its], G.at[:, own_cols], one_s.at[0], one_r.at[0], mate)
    for k in range(1, CHIPS):
        links.send(
            w.at[own_rows, lanes(chip_at(k), wide)], WC.at[chip, slab_rows],
            a2a_s.at[k], a2a_r.at[k], (z, chip_at(k) * 2 + core),
        )

    def got_one(ref, i):
        links.copy(ref, ref, one_s.at[i], one_r.at[i], mate).wait_recv()

    rate, residue = rate_ref[...], res_ref[...]
    xx = key[...].astype(f32) * val[...].astype(f32)
    interleave(xs, xx)
    local[0].wait()
    got_one(G.at[:, mate_cols], 0)
    first = Gather(links, G, g_send, g_recv, z, x, y, core)
    first.wave(0)
    sub = t // NSUB
    p = scan_states(xs, rate, False)
    states[0] = edge_of(p, False)
    for n in (1, 2, 3):
        links.send(
            states.at[0], state_got.at[0, n - 1], st_s.at[0, n - 1], st_r.at[0, n - 1], along(n)
        )
    local[1].wait()
    links.send(w, W2.at[lanes(core, c)], one_s.at[1], one_r.at[1], mate)
    first.wave(1)

    def carried(way):
        total = None
        for n in (1, 2, 3):
            here = state_got.at[way, n - 1]
            links.copy(here, here, st_s.at[way, n - 1], st_r.at[way, n - 1], mate).wait_recv()
            row = 3 * way + n - 1
            term = weights[row : row + 1, :] * jnp.exp(-rate * float(t * (n - 1))) * here[...]
            total = term if total is None else total + term
        return total

    start = entering_of(p, rate, sub, carried(0), False)
    forward_pass(xs, ys, hs, rate, residue, start)
    first.wave(2)
    cc = deinterleave(ys) + skip[...] * xx
    field[...] = cc
    prod[...] = (q[...].astype(f32) * cc).astype(bf16)
    links.send(prod.at[its], H.at[:, own_cols], one_s.at[2], one_r.at[2], mate)
    H[:, own_cols] = prod[mine, :]
    first.wave(3)
    local[2].wait()
    for k in range(1, CHIPS):
        here = WC.at[chip_at(CHIPS - k), slab_rows]
        links.copy(here, here, a2a_s.at[k], a2a_r.at[k], mate).wait_recv()
    for n in range(1, count):
        links.send(
            WC.at[:, slab_rows], WC.at[:, slab_rows], wz_s.at[n], wz_r.at[n], along(n)
        )
    got_one(H.at[:, mate_cols], 2)
    second = Gather(links, H, h_send, h_recv, z, x, y, core)
    first.wave(4)
    second.wave(0)
    first.wave(5)
    second.wave(1)
    first.wave(6)
    second.wave(2)

    got_one(W2.at[lanes(other, c)], 1)
    deep = n_out // 4
    acc = None
    for j in range(4):
        cols = pl.ds(j * deep, deep)
        term = lax.dot_general(
            G[:, cols], W2[:, cols], (((1,), (1,)), ((), ())), preferred_element_type=f32
        )
        acc = term if acc is None else acc + term
    is_first = core == 0
    dp[mine, :] = jnp.where(is_first, acc[:, :c], acc[:, c:])
    dp_send[...] = jnp.where(is_first, acc[:, c:], acc[:, :c])
    links.send(dp_send, dp.at[mine], one_s.at[3], one_r.at[3], mate)

    mate_t = H[:, mate_cols].T
    own_t = H[:, own_cols].T
    both = jnp.concatenate([mate_t, own_t], axis=0)
    block = n_out // 8
    for j in range(8):
        cols = pl.ds(j * block, block)
        r = jnp.dot(both, G[:, cols], preferred_element_type=f32)
        dw_send[:, cols] = r[:c].astype(bf16)
        dw_own[:, cols] = r[c:]
    links.send(dw_send, dw_got, one_s.at[4], one_r.at[4], mate)

    got_one(dp.at[its], 3)
    g = dp[...] * q[...].astype(f32)
    interleave(gs, g)
    p = scan_states(gs, rate, True)
    states[1] = edge_of(p, True)
    for n in (1, 2, 3):
        links.send(
            states.at[1], state_got.at[1, n - 1], st_s.at[1, n - 1], st_r.at[1, n - 1], along(-n)
        )
    second.wave(3)
    got_one(dw_got, 4)

    ways = [(way, lot) for lot in range(2) for way in range(2)]
    lot_rows = c // 2
    span = n_out // 2 // count

    def place(way, s):
        return pl.ds(pl.multiple_of(way * (n_out // 2) + s * span, span), span)

    def local_sum(way, lot, s):
        cols, rows = place(way, s), pl.ds(lot * lot_rows, lot_rows)
        return dw_own[rows, cols] + dw_got[rows, cols].astype(f32)

    def turn(way, k):
        sign = 1 - 2 * way
        return lax.rem(z + sign * k + 2 * count, count)

    def reduce_steps():
        for way, lot in ways:
            ring[way, lot, 0] = local_sum(way, lot, turn(way, -1)).astype(bf16)
        for step in range(count):
            for way, lot in ways:
                here = ring.at[way, lot, step]
                if step > 0:
                    links.copy(
                        here, here, rs_s.at[way, lot, step - 1], rs_r.at[way, lot, step - 1], mate
                    ).wait_recv()
                    s = turn(way, -1 - step)
                    total = (here[...].astype(f32) + local_sum(way, lot, s)).astype(bf16)
                    if step < count - 1:
                        here[...] = total
                    else:
                        dw_all[pl.ds(lot * lot_rows, lot_rows), place(way, s)] = total
                if step < count - 1:
                    links.send(
                        here, ring.at[way, lot, step + 1], rs_s.at[way, lot, step],
                        rs_r.at[way, lot, step], along(1 - 2 * way),
                    )
            if step < count - 1:
                yield
        for step in range(count):
            for way, lot in ways:
                here = dw_all.at[pl.ds(lot * lot_rows, lot_rows), place(way, turn(way, -step))]
                if step > 0:
                    links.copy(
                        here, here, ag_s.at[way, lot, step - 1], ag_r.at[way, lot, step - 1], mate
                    ).wait_recv()
                if step < count - 1:
                    links.send(
                        here, here, ag_s.at[way, lot, step], ag_r.at[way, lot, step],
                        along(1 - 2 * way),
                    )
            yield

    reduce = reduce_steps()
    next(reduce)
    start = entering_of(p, rate, sub, carried(1), True)
    result = []
    back = backward_pieces(xs, gs, ys, hs, rate, residue, start, 2, result)
    waves = [4, 5, 6]
    for step in range(5):
        next(back, None)
        next(reduce)
        if waves and step > 0:
            second.wave(waves.pop(0))

    dskip = jnp.sum(xx * g, axis=0, keepdims=True)
    for n in range(2):
        small_all[z, n * GROUP : (n + 1) * GROUP] = result[n]
        small_all[z, MODES + n * GROUP : MODES + (n + 1) * GROUP] = result[2 + n]
    small_all[z, 2 * MODES :] = jnp.broadcast_to(dskip, (GROUP, c))
    for n in range(1, count):
        links.send(small_all.at[z], small_all.at[z], sm_s.at[n], sm_r.at[n], along(n))
    next(reduce)
    dq[...] = (dp[...] * field[...]).astype(bf16)
    dm = deinterleave(ys) + skip[...] * g
    dk[...] = (dm * val[...].astype(f32)).astype(bf16)
    dv[...] = (dm * key[...].astype(f32)).astype(bf16)
    next(reduce)

    for n in range(1, count):
        here = WC.at[:, pl.ds(pl.multiple_of(core * c + turn(0, -n) * slab, slab), slab)]
        links.copy(here, here, wz_s.at[n], wz_r.at[n], mate).wait_recv()
    links.send(WC.at[:, lanes(core, c)], WC.at[:, lanes(core, c)], one_s.at[5], one_r.at[5], mate)
    next(reduce)
    got_one(WC.at[:, lanes(other, c)], 5)
    acc = None
    for j in range(4):
        per = CHIPS // 4
        term = jnp.dot(
            H[:, pl.ds(j * per * wide, per * wide)],
            WC[j * per : (j + 1) * per].reshape(per * wide, wide),
            preferred_element_type=f32,
        )
        acc = term if acc is None else acc + term
    out_all[mine, :] = jnp.where(is_first, acc[:, :c], acc[:, c:]).astype(bf16)
    out_send[...] = jnp.where(is_first, acc[:, c:], acc[:, :c]).astype(bf16)
    links.send(out_send, out_all.at[mine], one_s.at[6], one_r.at[6], mate)
    for _ in reduce:
        pass
    got_one(out_all.at[its], 6)
    out[...] = out_all[...]
    dw[...] = dw_all[...].astype(f32)
    for n in range(1, count):
        here = small_all.at[turn(0, -n)]
        links.copy(here, here, sm_s.at[n], sm_r.at[n], mate).wait_recv()
    total = small_all[0]
    for n in range(1, count):
        total = total + small_all[n]
    small[...] = total
    links.drain()


def shards(queries, keys, values, residue, rate, skip, w_out, lengths, d_out):
    t, c = queries.shape
    n_out = w_out.shape[1]
    place, count = lax.axis_index("pos"), lax.axis_size("pos")
    ends = jnp.cumsum(lengths)
    document = lambda b: jnp.sum((ends <= b).astype(jnp.int32))

    def weight(other):
        inside = (other >= 0) & (other < count)
        return jnp.where(inside & (document(other) == document(place)), 1.0, 0.0).astype(f32)

    weights = jnp.stack([weight(place + n) for n in (-1, -2, -3, 1, 2, 3)])
    weights = jnp.broadcast_to(weights[:, None], (6, c))
    thin = jax.ShapeDtypeStruct((t, c), bf16)
    rows = 2 * MODES + GROUP
    vmem, dma = pltpu.VMEM, pltpu.SemaphoreType.DMA
    wide, half = 2 * c, t // 2
    tall = vmem((t, c), f32)
    scratch = [
        vmem((half, n_out), bf16), vmem((half, n_out), bf16), vmem((wide, n_out), bf16),
        vmem((CHIPS, wide, wide), bf16), tall, tall, tall,
        vmem((t // NSUB, MODES, NSUB, c), f32), tall, tall, vmem((half, c), f32),
        vmem((t, c), bf16), vmem((half, c), bf16), vmem((t, c), bf16),
        vmem((2, MODES, c), f32), vmem((2, 3, MODES, c), f32), vmem((count, rows, c), f32),
        vmem((c, n_out), f32), vmem((c, n_out), bf16), vmem((c, n_out), bf16),
        vmem((2, 2, count, c // 2, n_out // 2 // count), bf16), vmem((c, n_out), bf16),
        dma((STREAMS, CHIPS, 2)), dma((STREAMS, CHIPS)), dma((STREAMS, CHIPS, 2)),
        dma((STREAMS, CHIPS)), dma((3,)), dma((7,)), dma((7,)), dma((CHIPS,)), dma((CHIPS,)),
        dma((count,)), dma((count,)), dma((2, 3)), dma((2, 3)), dma((count,)), dma((count,)),
        dma((2, 2, count)), dma((2, 2, count)), dma((2, 2, count)), dma((2, 2, count)),
    ]
    whole = pl.BlockSpec(memory_space=pltpu.VMEM)
    apart = pl.BlockSpec(memory_space=pl.ANY)
    out, dq, dk, dv, small, dw = pl.pallas_call(
        functools.partial(kernel, count),
        out_shape=(
            thin, thin, thin, thin, jax.ShapeDtypeStruct((rows, c), f32),
            jax.ShapeDtypeStruct((c, n_out), f32),
        ),
        in_specs=[whole] * 3 + [apart] * 2 + [whole] * 4,
        out_specs=(whole,) * 6,
        scratch_shapes=scratch,
        compiler_params=pltpu.CompilerParams(
            collective_id=0, has_side_effects=True, vmem_limit_bytes=60 * MIB
        ),
    )(queries, keys, values, w_out, d_out, rate.T, residue.T, skip[None, :], weights)
    return out, dq, dk, dv, small[:MODES].T, small[MODES : 2 * MODES].T, small[2 * MODES], dw


def solution(mesh):
    both, chan = P("pos", "ch"), P("ch", None)
    return jax.shard_map(
        shards,
        mesh=mesh,
        in_specs=(both, both, both, chan, chan, P("ch"), chan, P(), both),
        out_specs=(both, both, both, both, chan, chan, P("ch"), chan),
        check_vma=False,
    )
```

time: 302 us -> 131 us (0.43)
  the two profiles are of different devices: /device:TPU:1 before, /device:TPU:32 now
where the time goes in v2:
time: 131 us; the launch traced here: 130 us
  Pallas kernels  109 us (83%)
  local copies, waits for them, and re-layouts  11.4 us (9%)
  between operations  8.49 us (6%)
  other arithmetic  1.57 us (1%)
    pallas_call x1, Pallas kernels, shards(): pl.pallas_call(functools.partial(kernel, count), out_shape=(thin, thin, t...  109 us
    unnamed x7, local copies, waits for them, and re-layouts  8 us

profile of v2, /device:TPU:32, one launch (start us, length us, event | category | flops | bytes accessed | tf_op | source)
XLA Modules:
  0.0 130.1 jit_solution(6029997986603138118)
XLA Ops:
  0.7 0.8 reduce-window.9
  1.5 0.7 fusion.6
  10.0 0.1 stack.27
  10.1 0.7 broadcast_in_dim.10.weights
  10.8 108.7 %shard_map.152 = (bf16[1024,128]{1,0:T(8,128)(2,1)}, bf16[1024,128]{1,0:T(8,128)(2,1)}, bf16[1024,128]{1,0:T(8,128)(2,1)}, bf16[1024,128]{1,0:T(8,128)(2,1)}, f32[40,128]{1,0:T(8,128)}, /*index=5*/f32[128,4096]{1,0:T(8,128)}) custom-call(bf16[1024,128]{1,0:T(8,128)(2,1)} %q.1, bf16[1024,128]{1,0:T(8,128)(2,1)} %key.1, bf16[1024,128]{1,0:T(8,128)(2,1)} %val.1, ...), custom_call_target="tpu_custom_call" | custom-call | tf_op jit(solution)/shard_map/pallas_call | solution.py:485
  119.5 0.0 copy-start
  119.5 1.3 %slice_bitcast_fusion.2 = f32[128]{0:T(128)} fusion(f32[40,128]{1,0:T(8,128)} %get-tuple-element.18), kind=kLoop, calls=%fused_computation.16 | loop fusion | bytes 1024 | tf_op jit(solution)/shard_map/squeeze | solution.py:498
  120.8 1.3 %slice_bitcast_fusion = (f32[128,16]{0,1:T(8,128)}, f32[128,16]{0,1:T(8,128)}) fusion(f32[40,128]{1,0:T(8,128)} %get-tuple-element.18), kind=kLoop, calls=%fused_computation | loop fusion | bytes 32768 | tf_op jit(solution)/shard_map/transpose | solution.py:498
  122.1 1.7 %copy.22 = bf16[1024,128]{1,0:T(8,128)(2,1)} copy(bf16[1024,128]{1,0:T(8,128)(2,1)} %get-tuple-element.37) | data formatting | bytes 524288
  123.8 1.7 %copy.23 = bf16[1024,128]{1,0:T(8,128)(2,1)} copy(bf16[1024,128]{1,0:T(8,128)(2,1)} %get-tuple-element.38) | data formatting | bytes 524288
  125.5 1.7 %copy.24 = bf16[1024,128]{1,0:T(8,128)(2,1)} copy(bf16[1024,128]{1,0:T(8,128)(2,1)} %get-tuple-element.39) | data formatting | bytes 524288
  127.1 1.7 %copy.25 = bf16[1024,128]{1,0:T(8,128)(2,1)} copy(bf16[1024,128]{1,0:T(8,128)(2,1)} %get-tuple-element.40) | data formatting | bytes 524288
  128.8 0.0 copy-done
  128.8 1.3 %copy.26 = f32[128,4096]{1,0:T(8,128)} copy(f32[128,4096]{1,0:T(8,128)S(1)} %copy-done) | data formatting | bytes 4194304
Async XLA Ops:
  119.5 9.3 %copy-start = (f32[128,4096]{1,0:T(8,128)S(1)}, f32[128,4096]{1,0:T(8,128)}, u32[]{:S(2)}) copy-start(f32[128,4096]{1,0:T(8,128)} %get-tuple-element.44) | copy-start | bytes 6291460

commit v3 on v2

--- a/solution.py
+++ b/solution.py
@@ -16,6 +16,7 @@
 SIDE = 4
 CHIPS = SIDE * SIDE
 STREAMS = 4
+LOTS = 4
 MESH = pl.DeviceIdType.MESH
 MIB = 1024 * 1024
 
@@ -189,11 +190,75 @@
     return pl.ds(pl.multiple_of(i * width, width), width)
 
 
+class Ring:
+    def __init__(self, links, count, z, ch):
+        self.links, self.count, self.z, self.ch = links, count, z, ch
+        self.far = count // 2
+
+    def at(self, way, k):
+        return lax.rem(self.z + (1 - 2 * way) * k + 2 * self.count, self.count)
+
+    def next(self, way):
+        return (self.at(way, 1), self.ch)
+
+    def hops(self, way, lot):
+        return self.far if lot % 2 == way else self.count - 1 - self.far
+
+    def came(self, here, sems, way, lot, step):
+        self.links.copy(
+            here, here, sems[0].at[way, lot, step], sems[1].at[way, lot, step], self.next(way)
+        ).wait_recv()
+
+    def go(self, src, dst, sems, way, lot, step):
+        self.links.send(
+            src, dst, sems[0].at[way, lot, step], sems[1].at[way, lot, step], self.next(way)
+        )
+
+    def spread(self, region, lots, sems):
+        for step in range(self.far + 1):
+            for lot in range(lots):
+                for way in range(2):
+                    n = self.hops(way, lot)
+                    if step > n:
+                        continue
+                    here = region(self.at(way, -step), lot)
+                    if step > 0:
+                        self.came(here, sems, way, lot, step - 1)
+                    if step < n:
+                        self.go(here, here, sems, way, lot, step)
+            yield
+
+    def reduce(self, term, buf, lots, sems, keep):
+        for step in range(self.far):
+            for lot in range(lots):
+                for way in range(2):
+                    n = self.hops(way, lot)
+                    if step >= n:
+                        continue
+                    here = buf.at[way, lot, step]
+                    value = term(self.at(way, n - step), lot)
+                    if step > 0:
+                        self.came(here, sems, way, lot, step - 1)
+                        value = value + here[...].astype(f32)
+                    here[...] = value.astype(bf16)
+                    self.go(here, buf.at[way, lot, step + 1], sems, way, lot, step)
+            yield
+        for lot in range(lots):
+            value = term(self.z, lot)
+            for way in range(2):
+                n = self.hops(way, lot)
+                here = buf.at[way, lot, n]
+                self.came(here, sems, way, lot, n - 1)
+                value = value + here[...].astype(f32)
+            keep(lot, value)
+
+
 def kernel(
-    count, q, key, val, w, d_out, rate_ref, res_ref, skip, weights,
+    count, lengths, q_in, key_in, val_in, w, d_out, rate_in, res_in, skip_in,
     out, dq, dk, dv, small, dw,
+    q, key, val, rate_ref, res_ref, skip, dq_own, dk_own, dv_own,
     G, H, W2, WC, xs, gs, ys, hs, field, dp, dp_send, prod, out_send, out_all,
-    states, state_got, small_all, dw_own, dw_send, dw_got, ring, dw_all,
+    states, state_got, small_all, small_sum, dw_own, dw_send, dw_got, ring_buf, dw_all,
     g_send, g_recv, h_send, h_recv, loc, one_s, one_r, a2a_s, a2a_r, wz_s, wz_r,
     st_s, st_r, sm_s, sm_r, rs_s, rs_r, ag_s, ag_r,
 ):
@@ -226,11 +291,20 @@
     own_rows = pl.ds(pl.multiple_of(z * slab, slab), slab)
     slab_rows = pl.ds(pl.multiple_of(core * c + z * slab, slab), slab)
     local = [
-        pltpu.make_async_copy(d_out.at[mine], G.at[:, own_cols], loc.at[0]),
-        pltpu.make_async_copy(w, W2.at[lanes(core, c)], loc.at[1]),
-        pltpu.make_async_copy(
-            w.at[own_rows, lanes(chip, wide)], WC.at[chip, slab_rows], loc.at[2]
-        ),
+        pltpu.make_async_copy(src, dst, loc.at[n])
+        for n, (src, dst) in enumerate(
+            [
+                (d_out.at[mine], G.at[:, own_cols]),
+                (key_in, key),
+                (val_in, val),
+                (rate_in, rate_ref),
+                (res_in, res_ref),
+                (skip_in, skip),
+                (q_in, q),
+                (w.at[own_rows, lanes(chip, wide)], WC.at[chip, slab_rows]),
+                (w, W2.at[lanes(core, c)]),
+            ]
+        )
     ]
     for copy in local:
         copy.start()
@@ -247,6 +321,8 @@
     def got_one(ref, i):
         links.copy(ref, ref, one_s.at[i], one_r.at[i], mate).wait_recv()
 
+    for n in range(1, 6):
+        local[n].wait()
     rate, residue = rate_ref[...], res_ref[...]
     xx = key[...].astype(f32) * val[...].astype(f32)
     interleave(xs, xx)
@@ -261,17 +337,26 @@
         links.send(
             states.at[0], state_got.at[0, n - 1], st_s.at[0, n - 1], st_r.at[0, n - 1], along(n)
         )
-    local[1].wait()
     links.send(w, W2.at[lanes(core, c)], one_s.at[1], one_r.at[1], mate)
     first.wave(1)
+
+    def document(b):
+        end, before = lengths[0], jnp.int32(0)
+        for n in range(lengths.shape[0]):
+            before = before + jnp.where(end <= b, 1, 0)
+            if n + 1 < lengths.shape[0]:
+                end = end + lengths[n + 1]
+        return before
 
     def carried(way):
         total = None
         for n in (1, 2, 3):
             here = state_got.at[way, n - 1]
             links.copy(here, here, st_s.at[way, n - 1], st_r.at[way, n - 1], mate).wait_recv()
-            row = 3 * way + n - 1
-            term = weights[row : row + 1, :] * jnp.exp(-rate * float(t * (n - 1))) * here[...]
+            b = z + n if way else z - n
+            same = (b >= 0) & (b < count) & (document(b) == document(z))
+            decay = jnp.exp(-rate * float(t * (n - 1))) * jnp.where(same, 1.0, 0.0).astype(f32)
+            term = decay * here[...]
             total = term if total is None else total + term
         return total
 
@@ -280,40 +365,35 @@
     first.wave(2)
     cc = deinterleave(ys) + skip[...] * xx
     field[...] = cc
+    local[6].wait()
     prod[...] = (q[...].astype(f32) * cc).astype(bf16)
     links.send(prod.at[its], H.at[:, own_cols], one_s.at[2], one_r.at[2], mate)
     H[:, own_cols] = prod[mine, :]
     first.wave(3)
-    local[2].wait()
+    local[7].wait()
     for k in range(1, CHIPS):
         here = WC.at[chip_at(CHIPS - k), slab_rows]
         links.copy(here, here, a2a_s.at[k], a2a_r.at[k], mate).wait_recv()
-    for n in range(1, count):
-        links.send(
-            WC.at[:, slab_rows], WC.at[:, slab_rows], wz_s.at[n], wz_r.at[n], along(n)
-        )
+    ring = Ring(links, count, z, ch)
+    lot_chips = CHIPS // 2
+
+    def columns(s, lot):
+        rows = pl.ds(pl.multiple_of(core * c + s * slab, slab), slab)
+        return WC.at[lot * lot_chips : (lot + 1) * lot_chips, rows]
+
+    w_round = ring.spread(columns, 2, (wz_s, wz_r))
+    next(w_round)
     got_one(H.at[:, mate_cols], 2)
     second = Gather(links, H, h_send, h_recv, z, x, y, core)
     first.wave(4)
     second.wave(0)
+    next(w_round)
     first.wave(5)
     second.wave(1)
+    next(w_round)
     first.wave(6)
     second.wave(2)
-
-    got_one(W2.at[lanes(other, c)], 1)
-    deep = n_out // 4
-    acc = None
-    for j in range(4):
-        cols = pl.ds(j * deep, deep)
-        term = lax.dot_general(
-            G[:, cols], W2[:, cols], (((1,), (1,)), ((), ())), preferred_element_type=f32
-        )
-        acc = term if acc is None else acc + term
-    is_first = core == 0
-    dp[mine, :] = jnp.where(is_first, acc[:, :c], acc[:, c:])
-    dp_send[...] = jnp.where(is_first, acc[:, c:], acc[:, :c])
-    links.send(dp_send, dp.at[mine], one_s.at[3], one_r.at[3], mate)
+    next(w_round)
 
     mate_t = H[:, mate_cols].T
     own_t = H[:, own_cols].T
@@ -325,7 +405,45 @@
         dw_send[:, cols] = r[:c].astype(bf16)
         dw_own[:, cols] = r[c:]
     links.send(dw_send, dw_got, one_s.at[4], one_r.at[4], mate)
-
+    next(w_round)
+    links.send(WC.at[:, lanes(core, c)], WC.at[:, lanes(core, c)], one_s.at[5], one_r.at[5], mate)
+
+    local[8].wait()
+    got_one(W2.at[lanes(other, c)], 1)
+    deep = n_out // 4
+    acc = None
+    for j in range(4):
+        cols = pl.ds(j * deep, deep)
+        term = lax.dot_general(
+            G[:, cols], W2[:, cols], (((1,), (1,)), ((), ())), preferred_element_type=f32
+        )
+        acc = term if acc is None else acc + term
+    is_first = core == 0
+    dp[mine, :] = jnp.where(is_first, acc[:, :c], acc[:, c:])
+    dp_send[...] = jnp.where(is_first, acc[:, c:], acc[:, :c])
+    links.send(dp_send, dp.at[mine], one_s.at[3], one_r.at[3], mate)
+    got_one(dw_got, 4)
+
+    lot_rows = c // LOTS
+    span = n_out // count
+
+    def term(s, lot):
+        rows, cols = pl.ds(lot * lot_rows, lot_rows), lanes(s, span)
+        return dw_own[rows, cols] + dw_got[rows, cols].astype(f32)
+
+    def keep(lot, value):
+        dw_all[pl.ds(lot * lot_rows, lot_rows), lanes(z, span)] = value.astype(bf16)
+
+    def block_of(s, lot):
+        return dw_all.at[pl.ds(lot * lot_rows, lot_rows), lanes(s, span)]
+
+    def sums():
+        yield from ring.reduce(term, ring_buf, LOTS, (rs_s, rs_r), keep)
+        yield from ring.spread(block_of, LOTS, (ag_s, ag_r))
+
+    reduce = sums()
+    next(reduce)
+    second.wave(3)
     got_one(dp.at[its], 3)
     g = dp[...] * q[...].astype(f32)
     interleave(gs, g)
@@ -335,72 +453,21 @@
         links.send(
             states.at[1], state_got.at[1, n - 1], st_s.at[1, n - 1], st_r.at[1, n - 1], along(-n)
         )
-    second.wave(3)
-    got_one(dw_got, 4)
-
-    ways = [(way, lot) for lot in range(2) for way in range(2)]
-    lot_rows = c // 2
-    span = n_out // 2 // count
-
-    def place(way, s):
-        return pl.ds(pl.multiple_of(way * (n_out // 2) + s * span, span), span)
-
-    def local_sum(way, lot, s):
-        cols, rows = place(way, s), pl.ds(lot * lot_rows, lot_rows)
-        return dw_own[rows, cols] + dw_got[rows, cols].astype(f32)
-
-    def turn(way, k):
-        sign = 1 - 2 * way
-        return lax.rem(z + sign * k + 2 * count, count)
-
-    def reduce_steps():
-        for way, lot in ways:
-            ring[way, lot, 0] = local_sum(way, lot, turn(way, -1)).astype(bf16)
-        for step in range(count):
-            for way, lot in ways:
-                here = ring.at[way, lot, step]
-                if step > 0:
-                    links.copy(
-                        here, here, rs_s.at[way, lot, step - 1], rs_r.at[way, lot, step - 1], mate
-                    ).wait_recv()
-                    s = turn(way, -1 - step)
-                    total = (here[...].astype(f32) + local_sum(way, lot, s)).astype(bf16)
-                    if step < count - 1:
-                        here[...] = total
-                    else:
-                        dw_all[pl.ds(lot * lot_rows, lot_rows), place(way, s)] = total
-                if step < count - 1:
-                    links.send(
-                        here, ring.at[way, lot, step + 1], rs_s.at[way, lot, step],
-                        rs_r.at[way, lot, step], along(1 - 2 * way),
-                    )
-            if step < count - 1:
-                yield
-        for step in range(count):
-            for way, lot in ways:
-                here = dw_all.at[pl.ds(lot * lot_rows, lot_rows), place(way, turn(way, -step))]
-                if step > 0:
-                    links.copy(
-                        here, here, ag_s.at[way, lot, step - 1], ag_r.at[way, lot, step - 1], mate
-                    ).wait_recv()
-                if step < count - 1:
-                    links.send(
-                        here, here, ag_s.at[way, lot, step], ag_r.at[way, lot, step],
-                        along(1 - 2 * way),
-                    )
-            yield
-
-    reduce = reduce_steps()
-    next(reduce)
+    next(reduce)
+    second.wave(4)
     start = entering_of(p, rate, sub, carried(1), True)
     result = []
     back = backward_pieces(xs, gs, ys, hs, rate, residue, start, 2, result)
-    waves = [4, 5, 6]
-    for step in range(5):
-        next(back, None)
-        next(reduce)
-        if waves and step > 0:
-            second.wave(waves.pop(0))
+    next(back)
+    next(reduce)
+    second.wave(5)
+    next(back)
+    next(reduce)
+    second.wave(6)
+    next(back)
+    next(reduce)
+    next(back)
+    next(back, None)
 
     dskip = jnp.sum(xx * g, axis=0, keepdims=True)
     for n in range(2):
@@ -410,75 +477,86 @@
     for n in range(1, count):
         links.send(small_all.at[z], small_all.at[z], sm_s.at[n], sm_r.at[n], along(n))
     next(reduce)
-    dq[...] = (dp[...] * field[...]).astype(bf16)
+    dq_own[...] = (dp[...] * field[...]).astype(bf16)
     dm = deinterleave(ys) + skip[...] * g
-    dk[...] = (dm * val[...].astype(f32)).astype(bf16)
-    dv[...] = (dm * key[...].astype(f32)).astype(bf16)
-    next(reduce)
-
-    for n in range(1, count):
-        here = WC.at[:, pl.ds(pl.multiple_of(core * c + turn(0, -n) * slab, slab), slab)]
-        links.copy(here, here, wz_s.at[n], wz_r.at[n], mate).wait_recv()
-    links.send(WC.at[:, lanes(core, c)], WC.at[:, lanes(core, c)], one_s.at[5], one_r.at[5], mate)
-    next(reduce)
+    dk_own[...] = (dm * val[...].astype(f32)).astype(bf16)
+    dv_own[...] = (dm * key[...].astype(f32)).astype(bf16)
+    done = [
+        pltpu.make_async_copy(src, dst, loc.at[n])
+        for n, (src, dst) in enumerate(
+            [(dq_own, dq), (dk_own, dk), (dv_own, dv), (small_sum, small), (out_all, out), (dw_all, dw)]
+        )
+    ]
+    for n in range(3):
+        done[n].start()
+    next(reduce)
+
     got_one(WC.at[:, lanes(other, c)], 5)
     acc = None
     for j in range(4):
         per = CHIPS // 4
-        term = jnp.dot(
+        part = jnp.dot(
             H[:, pl.ds(j * per * wide, per * wide)],
             WC[j * per : (j + 1) * per].reshape(per * wide, wide),
             preferred_element_type=f32,
         )
-        acc = term if acc is None else acc + term
+        acc = part if acc is None else acc + part
     out_all[mine, :] = jnp.where(is_first, acc[:, :c], acc[:, c:]).astype(bf16)
     out_send[...] = jnp.where(is_first, acc[:, c:], acc[:, :c]).astype(bf16)
     links.send(out_send, out_all.at[mine], one_s.at[6], one_r.at[6], mate)
     for _ in reduce:
         pass
-    got_one(out_all.at[its], 6)
-    out[...] = out_all[...]
-    dw[...] = dw_all[...].astype(f32)
+    done[5].start()
     for n in range(1, count):
-        here = small_all.at[turn(0, -n)]
+        here = small_all.at[ring.at(0, -n)]
         links.copy(here, here, sm_s.at[n], sm_r.at[n], mate).wait_recv()
     total = small_all[0]
     for n in range(1, count):
         total = total + small_all[n]
-    small[...] = total
+    small_sum[...] = total
+    done[3].start()
+    got_one(out_all.at[its], 6)
+    done[4].start()
     links.drain()
+    for copy in done:
+        copy.wait()
+
+
+def finish(out_in, dq_in, dk_in, dv_in, small, dw_in, out, dq, dk, dv, dres, drate, dskip, dw):
+    out[...] = out_in[...]
+    dq[...] = dq_in[...]
+    dk[...] = dk_in[...]
+    dv[...] = dv_in[...]
+    dres[...] = small[:MODES]
+    drate[...] = small[MODES : 2 * MODES]
+    dskip[...] = small[2 * MODES : 2 * MODES + 1]
+    dw[...] = dw_in[...].astype(f32)
 
 
 def shards(queries, keys, values, residue, rate, skip, w_out, lengths, d_out):
     t, c = queries.shape
     n_out = w_out.shape[1]
-    place, count = lax.axis_index("pos"), lax.axis_size("pos")
-    ends = jnp.cumsum(lengths)
-    document = lambda b: jnp.sum((ends <= b).astype(jnp.int32))
-
-    def weight(other):
-        inside = (other >= 0) & (other < count)
-        return jnp.where(inside & (document(other) == document(place)), 1.0, 0.0).astype(f32)
-
-    weights = jnp.stack([weight(place + n) for n in (-1, -2, -3, 1, 2, 3)])
-    weights = jnp.broadcast_to(weights[:, None], (6, c))
+    count = lax.axis_size("pos")
     thin = jax.ShapeDtypeStruct((t, c), bf16)
     rows = 2 * MODES + GROUP
     vmem, dma = pltpu.VMEM, pltpu.SemaphoreType.DMA
-    wide, half = 2 * c, t // 2
-    tall = vmem((t, c), f32)
+    wide, half, far = 2 * c, t // 2, count // 2
+    tall, short = vmem((t, c), f32), vmem((t, c), bf16)
+    few = vmem((MODES, c), f32)
     scratch = [
+        short, short, short, few, few, vmem((1, c), f32), short, short, short,
         vmem((half, n_out), bf16), vmem((half, n_out), bf16), vmem((wide, n_out), bf16),
         vmem((CHIPS, wide, wide), bf16), tall, tall, tall,
         vmem((t // NSUB, MODES, NSUB, c), f32), tall, tall, vmem((half, c), f32),
-        vmem((t, c), bf16), vmem((half, c), bf16), vmem((t, c), bf16),
+        short, vmem((half, c), bf16), short,
         vmem((2, MODES, c), f32), vmem((2, 3, MODES, c), f32), vmem((count, rows, c), f32),
+        vmem((rows, c), f32),
         vmem((c, n_out), f32), vmem((c, n_out), bf16), vmem((c, n_out), bf16),
-        vmem((2, 2, count, c // 2, n_out // 2 // count), bf16), vmem((c, n_out), bf16),
+        vmem((2, LOTS, far + 1, c // LOTS, n_out // count), bf16), vmem((c, n_out), bf16),
         dma((STREAMS, CHIPS, 2)), dma((STREAMS, CHIPS)), dma((STREAMS, CHIPS, 2)),
-        dma((STREAMS, CHIPS)), dma((3,)), dma((7,)), dma((7,)), dma((CHIPS,)), dma((CHIPS,)),
-        dma((count,)), dma((count,)), dma((2, 3)), dma((2, 3)), dma((count,)), dma((count,)),
-        dma((2, 2, count)), dma((2, 2, count)), dma((2, 2, count)), dma((2, 2, count)),
+        dma((STREAMS, CHIPS)), dma((9,)), dma((7,)), dma((7,)), dma((CHIPS,)), dma((CHIPS,)),
+        dma((2, 2, far)), dma((2, 2, far)), dma((2, 3)), dma((2, 3)), dma((count,)), dma((count,)),
+        dma((2, LOTS, far)), dma((2, LOTS, far)), dma((2, LOTS, far)), dma((2, LOTS, far)),
     ]
     whole = pl.BlockSpec(memory_space=pltpu.VMEM)
     apart = pl.BlockSpec(memory_space=pl.ANY)
@@ -486,16 +564,27 @@
         functools.partial(kernel, count),
         out_shape=(
             thin, thin, thin, thin, jax.ShapeDtypeStruct((rows, c), f32),
-            jax.ShapeDtypeStruct((c, n_out), f32),
+            jax.ShapeDtypeStruct((c, n_out), bf16),
         ),
-        in_specs=[whole] * 3 + [apart] * 2 + [whole] * 4,
-        out_specs=(whole,) * 6,
+        in_specs=[pl.BlockSpec(memory_space=pltpu.SMEM)] + [apart] * 8,
+        out_specs=(apart,) * 6,
         scratch_shapes=scratch,
         compiler_params=pltpu.CompilerParams(
             collective_id=0, has_side_effects=True, vmem_limit_bytes=60 * MIB
         ),
-    )(queries, keys, values, w_out, d_out, rate.T, residue.T, skip[None, :], weights)
-    return out, dq, dk, dv, small[:MODES].T, small[MODES : 2 * MODES].T, small[2 * MODES], dw
+    )(lengths, queries, keys, values, w_out, d_out, rate.T, residue.T, skip[None, :])
+    state = jax.ShapeDtypeStruct((MODES, c), f32)
+    out, dq, dk, dv, dres, drate, dskip, dw = pl.pallas_call(
+        finish,
+        out_shape=(
+            thin, thin, thin, thin, state, state, jax.ShapeDtypeStruct((1, c), f32),
+            jax.ShapeDtypeStruct((c, n_out), f32),
+        ),
+        in_specs=[whole] * 6,
+        out_specs=(whole,) * 8,
+        compiler_params=pltpu.CompilerParams(vmem_limit_bytes=60 * MIB),
+    )(out, dq, dk, dv, small, dw)
+    return out, dq, dk, dv, dres.T, drate.T, dskip[0], dw
 
 
 def solution(mesh):

time: 131 us -> 94.4 us (0.72)
  the two profiles are of different devices: /device:TPU:32 before, /device:TPU:1 now
where the time goes in v3:
time: 94.4 us; the launch traced here: 93.5 us
  Pallas kernels  92.9 us (98%)
    pallas_call x1, Pallas kernels, shards(): pl.pallas_call(functools.partial(kernel, count), out_shape=(thin, thin, t...  89.6 us
    pallas_call x1, Pallas kernels, shards(): pl.pallas_call(finish, out_shape=(thin, thin, thin, thin, state, state, j...  3.27 us

profile of v3, /device:TPU:1, one launch (start us, length us, event | category | flops | bytes accessed | tf_op | source)
XLA Modules:
  0.0 93.5 jit_solution(12956543193175279937)
XLA Ops:
  0.6 89.6 %shard_map.152 = (bf16[1024,128]{1,0:T(8,128)(2,1)}, bf16[1024,128]{1,0:T(8,128)(2,1)}, bf16[1024,128]{1,0:T(8,128)(2,1)}, bf16[1024,128]{1,0:T(8,128)(2,1)}, f3...) custom-call(s32[3]{0:T(128)} %lengths.1, bf16[1024,128]{1,0:T(8,128)(2,1)} %q_in.1, bf16[1024,128]{1,0:T(8,128)(2,1)} %key_in.1, ...), custom_call_target="tpu_custom_call" | custom-call | tf_op jit(solution)/shard_map/pallas_call | solution.py:563
  90.3 3.3 %shard_map.153 = (bf16[1024,128]{1,0:T(8,128)(2,1)}, bf16[1024,128]{1,0:T(8,128)(2,1)}, bf16[1024,128]{1,0:T(8,128)(2,1)}, bf16[1024,128]{1,0:T(8,128)(2,1)}, f3...) custom-call(bf16[1024,128]{1,0:T(8,128)(2,1)} %get-tuple-element.22.out_in, ...), custom_call_target="tpu_custom_call" | custom-call | tf_op jit(solution)/shard_map/pallas_call | solution.py:577

commit v4 on v3

--- a/solution.py
+++ b/solution.py
@@ -15,8 +15,6 @@
 UNROLL = 4
 SIDE = 4
 CHIPS = SIDE * SIDE
-STREAMS = 4
-LOTS = 4
 MESH = pl.DeviceIdType.MESH
 MIB = 1024 * 1024
 
@@ -136,54 +134,78 @@
         self.sent = []
 
 
+NEAR = (-1, 0, 1, 2)
+FULL, LOW, HIGH = range(3)
+KEYS = [(1, 0, FULL), (-1, 0, FULL), (2, 0, LOW), (2, 0, HIGH)]
+for i in (0, 1, -1, 2):
+    KEYS += [(i, 1, FULL), (i, -1, FULL), (i, 2, LOW), (i, 2, HIGH)]
+OFFSETS = sorted([(i, j) for i in NEAR for j in NEAR], key=lambda o: abs(o[0]) + abs(o[1]))
+SCHEDULE = (
+    "tw", "g0", "f2", "t0w", "g1", "p0", "f3", "t01w", "s0", "f4", "g2", "p1", "t01w", "bs",
+    "t012w", "s1", "be", "t012w", "b", "b", "t012w", "b", "b", "t012", "s2", "b", "bz", "t012",
+    "t012", "t012", "s3", "t012", "o0", "t012", "s4", "t012", "o1",
+)
+GROUPS = [((0, 3), (3, 5)), ((5, 8), (8, 11)), ((11, 13), (13, 16))]
+
+
 class Gather:
     def __init__(self, links, buf, send, recv, z, x, y, core):
         self.links, self.buf, self.send_sem, self.recv_sem = links, buf, send, recv
         self.z, self.at, self.core = z, (x, y), core
 
-    def axes(self, s):
-        return (0, 1, 1 - 2 * (s % 2)) if s < 2 else (1, 0, 1 - 2 * (s % 2))
-
-    def region(self, s, i, j):
-        a, b, sign = self.axes(s)
+    def region(self, kind, i, j, part):
         at = list(self.at)
-        at[a] = lax.rem(at[a] - sign * i + SIDE, SIDE)
-        at[b] = lax.rem(at[b] - sign * j + SIDE, SIDE)
-        chip = at[0] * SIDE + at[1]
-        rows = self.buf.shape[0] // STREAMS
+        at[kind] = lax.rem(at[kind] + i + SIDE, SIDE)
+        at[1 - kind] = lax.rem(at[1 - kind] + j + SIDE, SIDE)
+        rows = self.buf.shape[0] // 2
+        start = kind * rows + (rows // 2 if part == HIGH else 0)
         wide = self.buf.shape[1] // CHIPS
-        return self.buf.at[pl.ds(s * rows, rows), pl.ds(pl.multiple_of(chip * wide, wide), wide)]
-
-    def device(self, s, second):
-        sign = self.axes(s)[2]
-        axis = self.axes(s)[1 if second else 0]
+        return self.buf.at[
+            pl.ds(start, rows if part == FULL else rows // 2), lanes(at[0] * SIDE + at[1], wide)
+        ]
+
+    def device(self, axis, sign):
         at = list(self.at)
         at[axis] = lax.rem(at[axis] + sign + SIDE, SIDE)
         return (self.z, (at[0] * SIDE + at[1]) * 2 + self.core)
 
-    def copy(self, s, i, j, second):
-        here = self.region(s, i, j)
-        k = i * SIDE + j
-        return (
-            here, here, self.send_sem.at[s, k, second],
-            self.recv_sem.at[s, k + (1 if second else SIDE)], self.device(s, second),
-        )
+    def send(self, kind, i, j, part):
+        n = KEYS.index((i, j, part))
+        step = {LOW: 1, HIGH: -1}.get(part, 0)
+        away = j if j else i
+        sign = -step if step else -away
+        here = self.region(kind, i, step, part) if j else self.region(kind, step, 0, part)
+        self.links.send(
+            here, here, self.send_sem.at[kind, n], self.recv_sem.at[kind, n],
+            self.device(1 - kind if j else kind, sign),
+        )
+
+    def got(self, kind, i, j, part):
+        n = KEYS.index((i, j, part))
+        here = self.region(kind, i, j, part)
+        self.links.copy(
+            here, here, self.send_sem.at[kind, n], self.recv_sem.at[kind, n], self.device(kind, 1)
+        ).wait_recv()
 
     def wave(self, k):
-        for i in range(min(k, SIDE - 1), -1, -1):
-            j = k - i
-            if j >= SIDE:
-                continue
-            for s in range(STREAMS):
-                if k > 0:
-                    second = 1 if j else 0
-                    came = self.copy(s, i - (1 - second), j - second, second)
-                    here = self.region(s, i, j)
-                    self.links.copy(here, here, came[2], came[3], came[4]).wait_recv()
-                if j == 0 and i < SIDE - 1:
-                    self.links.send(*self.copy(s, i, j, 0))
-                if j < SIDE - 1:
-                    self.links.send(*self.copy(s, i, j, 1))
+        for i in (1, -1, 2, 0):
+            for j in (0, 1, -1, 2):
+                if abs(i) + abs(j) != k:
+                    continue
+                for kind in range(2):
+                    for part in (LOW, HIGH) if 2 in (i, j) and (j == 2 or j == 0) else (FULL,):
+                        if k > 0:
+                            self.got(kind, i, j, part)
+                    if k == 0:
+                        self.send(kind, 1, 0, FULL)
+                        self.send(kind, -1, 0, FULL)
+                    elif j == 0 and abs(i) == 1:
+                        self.send(kind, 2, 0, LOW if i == 1 else HIGH)
+                    if j == 0:
+                        self.send(kind, i, 1, FULL)
+                        self.send(kind, i, -1, FULL)
+                    elif abs(j) == 1:
+                        self.send(kind, i, 2, LOW if j == 1 else HIGH)
 
 
 def lanes(i, width):
@@ -228,26 +250,26 @@
                         self.go(here, here, sems, way, lot, step)
             yield
 
-    def reduce(self, term, buf, lots, sems, keep):
+    def reduce(self, term, slot, lots, sems, keep):
         for step in range(self.far):
             for lot in range(lots):
                 for way in range(2):
                     n = self.hops(way, lot)
                     if step >= n:
                         continue
-                    here = buf.at[way, lot, step]
+                    here = slot(way, lot, step)
                     value = term(self.at(way, n - step), lot)
                     if step > 0:
                         self.came(here, sems, way, lot, step - 1)
                         value = value + here[...].astype(f32)
                     here[...] = value.astype(bf16)
-                    self.go(here, buf.at[way, lot, step + 1], sems, way, lot, step)
+                    self.go(here, slot(way, lot, step + 1), sems, way, lot, step)
             yield
         for lot in range(lots):
             value = term(self.z, lot)
             for way in range(2):
                 n = self.hops(way, lot)
-                here = buf.at[way, lot, n]
+                here = slot(way, lot, n)
                 self.came(here, sems, way, lot, n - 1)
                 value = value + here[...].astype(f32)
             keep(lot, value)
@@ -260,7 +282,7 @@
     G, H, W2, WC, xs, gs, ys, hs, field, dp, dp_send, prod, out_send, out_all,
     states, state_got, small_all, small_sum, dw_own, dw_send, dw_got, ring_buf, dw_all,
     g_send, g_recv, h_send, h_recv, loc, one_s, one_r, a2a_s, a2a_r, wz_s, wz_r,
-    st_s, st_r, sm_s, sm_r, rs_s, rs_r, ag_s, ag_r,
+    st_s, st_r, sm_s, sm_r, rs_s, rs_r, ag_s, ag_r, acc_ref, dw_sem,
 ):
     z, ch = lax.axis_index("pos"), lax.axis_index("ch")
     core, chip = lax.rem(ch, 2), lax.div(ch, 2)
@@ -338,7 +360,6 @@
             states.at[0], state_got.at[0, n - 1], st_s.at[0, n - 1], st_r.at[0, n - 1], along(n)
         )
     links.send(w, W2.at[lanes(core, c)], one_s.at[1], one_r.at[1], mate)
-    first.wave(1)
 
     def document(b):
         end, before = lengths[0], jnp.int32(0)
@@ -362,18 +383,13 @@
 
     start = entering_of(p, rate, sub, carried(0), False)
     forward_pass(xs, ys, hs, rate, residue, start)
-    first.wave(2)
+    first.wave(1)
     cc = deinterleave(ys) + skip[...] * xx
     field[...] = cc
     local[6].wait()
     prod[...] = (q[...].astype(f32) * cc).astype(bf16)
     links.send(prod.at[its], H.at[:, own_cols], one_s.at[2], one_r.at[2], mate)
     H[:, own_cols] = prod[mine, :]
-    first.wave(3)
-    local[7].wait()
-    for k in range(1, CHIPS):
-        here = WC.at[chip_at(CHIPS - k), slab_rows]
-        links.copy(here, here, a2a_s.at[k], a2a_r.at[k], mate).wait_recv()
     ring = Ring(links, count, z, ch)
     lot_chips = CHIPS // 2
 
@@ -381,132 +397,174 @@
         rows = pl.ds(pl.multiple_of(core * c + s * slab, slab), slab)
         return WC.at[lot * lot_chips : (lot + 1) * lot_chips, rows]
 
-    w_round = ring.spread(columns, 2, (wz_s, wz_r))
-    next(w_round)
     got_one(H.at[:, mate_cols], 2)
     second = Gather(links, H, h_send, h_recv, z, x, y, core)
-    first.wave(4)
-    second.wave(0)
-    next(w_round)
-    first.wave(5)
-    second.wave(1)
-    next(w_round)
-    first.wave(6)
-    second.wave(2)
-    next(w_round)
-
-    mate_t = H[:, mate_cols].T
-    own_t = H[:, own_cols].T
-    both = jnp.concatenate([mate_t, own_t], axis=0)
-    block = n_out // 8
-    for j in range(8):
-        cols = pl.ds(j * block, block)
-        r = jnp.dot(both, G[:, cols], preferred_element_type=f32)
-        dw_send[:, cols] = r[:c].astype(bf16)
-        dw_own[:, cols] = r[c:]
-    links.send(dw_send, dw_got, one_s.at[4], one_r.at[4], mate)
-    next(w_round)
-    links.send(WC.at[:, lanes(core, c)], WC.at[:, lanes(core, c)], one_s.at[5], one_r.at[5], mate)
-
-    local[8].wait()
-    got_one(W2.at[lanes(other, c)], 1)
-    deep = n_out // 4
-    acc = None
-    for j in range(4):
-        cols = pl.ds(j * deep, deep)
-        term = lax.dot_general(
-            G[:, cols], W2[:, cols], (((1,), (1,)), ((), ())), preferred_element_type=f32
-        )
-        acc = term if acc is None else acc + term
+
+    def chip_of(p):
+        i, j = OFFSETS[p]
+        return lax.rem(x + i + SIDE, SIDE) * SIDE + lax.rem(y + j + SIDE, SIDE)
+
+    both = jnp.concatenate([H[:, mate_cols].T, H[:, own_cols].T], axis=0)
+
+    def packed(first_one, last):
+        return pl.ds(first_one * wide, (last - first_one) * wide)
+
+    def weight_part(group):
+        lots = GROUPS[group]
+        for p in range(lots[0][0], lots[-1][1]):
+            r = jnp.dot(both, G[:, lanes(chip_of(p), wide)], preferred_element_type=f32)
+            dw_send[:, packed(p, p + 1)] = r[:c].astype(bf16)
+            dw_own[:, packed(p, p + 1)] = r[c:]
+        cols = packed(lots[0][0], lots[-1][1])
+        links.send(
+            dw_send.at[:, cols], dw_got.at[:, cols], one_s.at[7 + group], one_r.at[7 + group], mate
+        )
+
+    def sums(group):
+        lots = GROUPS[group]
+        cols = packed(lots[0][0], lots[-1][1])
+        got_one(dw_got.at[:, cols], 7 + group)
+
+        def term(s, lot):
+            rows, part = lanes(s, slab), packed(*lots[lot])
+            return dw_own[rows, part] + dw_got[rows, part].astype(f32)
+
+        def slot(way, lot, step):
+            return ring_buf.at[
+                group, way, lot, step, :, pl.ds(0, (lots[lot][1] - lots[lot][0]) * wide)
+            ]
+
+        def keep(lot, value):
+            dw_all[lanes(z, slab), packed(*lots[lot])] = value.astype(bf16)
+
+        def block_of(s, lot):
+            return dw_all.at[lanes(s, slab), packed(*lots[lot])]
+
+        yield from ring.reduce(term, slot, 2, (rs_s.at[group], rs_r.at[group]), keep)
+        yield from ring.spread(block_of, 2, (ag_s.at[group], ag_r.at[group]))
+        for p in range(lots[0][0], lots[-1][1]):
+            copy = pltpu.make_async_copy(
+                dw_all.at[:, packed(p, p + 1)], dw.at[:, lanes(chip_of(p), wide)], dw_sem.at[p]
+            )
+            copy.start()
+            done.append(copy)
+
+    done = []
+
+    def weight_columns():
+        local[7].wait()
+        for k in range(1, CHIPS):
+            here = WC.at[chip_at(CHIPS - k), slab_rows]
+            links.copy(here, here, a2a_s.at[k], a2a_r.at[k], mate).wait_recv()
+        yield from ring.spread(columns, 2, (wz_s, wz_r))
+        links.send(
+            WC.at[:, lanes(core, c)], WC.at[:, lanes(core, c)], one_s.at[5], one_r.at[5], mate
+        )
+
+    rounds = {"w": weight_columns(), "0": sums(0), "1": sums(1), "2": sums(2)}
+
+    def product_part(lo, hi, acc):
+        for p in range(lo, hi):
+            cols = lanes(chip_of(p), wide)
+            part = lax.dot_general(
+                G[:, cols], W2[:, cols], (((1,), (1,)), ((), ())), preferred_element_type=f32
+            )
+            acc = part if acc is None else acc + part
+        return acc
+
+    def out_part(lo, hi, acc):
+        for p in range(lo, hi):
+            part = jnp.dot(
+                H[:, lanes(chip_of(p), wide)], WC[chip_of(p)], preferred_element_type=f32
+            )
+            acc = part if acc is None else acc + part
+        return acc
+
+    near = GROUPS[1][-1][1]
     is_first = core == 0
-    dp[mine, :] = jnp.where(is_first, acc[:, :c], acc[:, c:])
-    dp_send[...] = jnp.where(is_first, acc[:, c:], acc[:, :c])
-    links.send(dp_send, dp.at[mine], one_s.at[3], one_r.at[3], mate)
-    got_one(dw_got, 4)
-
-    lot_rows = c // LOTS
-    span = n_out // count
-
-    def term(s, lot):
-        rows, cols = pl.ds(lot * lot_rows, lot_rows), lanes(s, span)
-        return dw_own[rows, cols] + dw_got[rows, cols].astype(f32)
-
-    def keep(lot, value):
-        dw_all[pl.ds(lot * lot_rows, lot_rows), lanes(z, span)] = value.astype(bf16)
-
-    def block_of(s, lot):
-        return dw_all.at[pl.ds(lot * lot_rows, lot_rows), lanes(s, span)]
-
-    def sums():
-        yield from ring.reduce(term, ring_buf, LOTS, (rs_s, rs_r), keep)
-        yield from ring.spread(block_of, LOTS, (ag_s, ag_r))
-
-    reduce = sums()
-    next(reduce)
-    second.wave(3)
-    got_one(dp.at[its], 3)
-    g = dp[...] * q[...].astype(f32)
-    interleave(gs, g)
-    p = scan_states(gs, rate, True)
-    states[1] = edge_of(p, True)
-    for n in (1, 2, 3):
-        links.send(
-            states.at[1], state_got.at[1, n - 1], st_s.at[1, n - 1], st_r.at[1, n - 1], along(-n)
-        )
-    next(reduce)
-    second.wave(4)
-    start = entering_of(p, rate, sub, carried(1), True)
-    result = []
-    back = backward_pieces(xs, gs, ys, hs, rate, residue, start, 2, result)
-    next(back)
-    next(reduce)
-    second.wave(5)
-    next(back)
-    next(reduce)
-    second.wave(6)
-    next(back)
-    next(reduce)
-    next(back)
-    next(back, None)
-
-    dskip = jnp.sum(xx * g, axis=0, keepdims=True)
-    for n in range(2):
-        small_all[z, n * GROUP : (n + 1) * GROUP] = result[n]
-        small_all[z, MODES + n * GROUP : MODES + (n + 1) * GROUP] = result[2 + n]
-    small_all[z, 2 * MODES :] = jnp.broadcast_to(dskip, (GROUP, c))
-    for n in range(1, count):
-        links.send(small_all.at[z], small_all.at[z], sm_s.at[n], sm_r.at[n], along(n))
-    next(reduce)
-    dq_own[...] = (dp[...] * field[...]).astype(bf16)
-    dm = deinterleave(ys) + skip[...] * g
-    dk_own[...] = (dm * val[...].astype(f32)).astype(bf16)
-    dv_own[...] = (dm * key[...].astype(f32)).astype(bf16)
-    done = [
-        pltpu.make_async_copy(src, dst, loc.at[n])
-        for n, (src, dst) in enumerate(
-            [(dq_own, dq), (dk_own, dk), (dv_own, dv), (small_sum, small), (out_all, out), (dw_all, dw)]
-        )
-    ]
-    for n in range(3):
-        done[n].start()
-    next(reduce)
-
-    got_one(WC.at[:, lanes(other, c)], 5)
-    acc = None
-    for j in range(4):
-        per = CHIPS // 4
-        part = jnp.dot(
-            H[:, pl.ds(j * per * wide, per * wide)],
-            WC[j * per : (j + 1) * per].reshape(per * wide, wide),
-            preferred_element_type=f32,
-        )
-        acc = part if acc is None else acc + part
-    out_all[mine, :] = jnp.where(is_first, acc[:, :c], acc[:, c:]).astype(bf16)
-    out_send[...] = jnp.where(is_first, acc[:, c:], acc[:, :c]).astype(bf16)
-    links.send(out_send, out_all.at[mine], one_s.at[6], one_r.at[6], mate)
-    for _ in reduce:
-        pass
-    done[5].start()
+
+    def product_near():
+        local[8].wait()
+        got_one(W2.at[lanes(other, c)], 1)
+        acc_ref[...] = product_part(0, near, None)
+
+    def product_far():
+        acc = product_part(near, CHIPS, acc_ref[...])
+        dp[mine, :] = jnp.where(is_first, acc[:, :c], acc[:, c:])
+        dp_send[...] = jnp.where(is_first, acc[:, c:], acc[:, :c])
+        links.send(dp_send, dp.at[mine], one_s.at[3], one_r.at[3], mate)
+
+    kept = {}
+
+    def back_states():
+        got_one(dp.at[its], 3)
+        g = dp[...] * q[...].astype(f32)
+        interleave(gs, g)
+        kept["g"] = g
+        kept["p"] = scan_states(gs, rate, True)
+        states[1] = edge_of(kept["p"], True)
+        for n in (1, 2, 3):
+            links.send(
+                states.at[1], state_got.at[1, n - 1], st_s.at[1, n - 1], st_r.at[1, n - 1], along(-n)
+            )
+
+    def back_start():
+        start = entering_of(kept["p"], rate, sub, carried(1), True)
+        kept["sums"] = []
+        kept["back"] = backward_pieces(xs, gs, ys, hs, rate, residue, start, 2, kept["sums"])
+
+    def back_piece():
+        next(kept["back"], None)
+
+    def back_end():
+        g, result = kept["g"], kept["sums"]
+        dskip = jnp.sum(xx * g, axis=0, keepdims=True)
+        for n in range(2):
+            small_all[z, n * GROUP : (n + 1) * GROUP] = result[n]
+            small_all[z, MODES + n * GROUP : MODES + (n + 1) * GROUP] = result[2 + n]
+        small_all[z, 2 * MODES :] = jnp.broadcast_to(dskip, (GROUP, c))
+        for n in range(1, count):
+            links.send(small_all.at[z], small_all.at[z], sm_s.at[n], sm_r.at[n], along(n))
+        dq_own[...] = (dp[...] * field[...]).astype(bf16)
+        dm = deinterleave(ys) + skip[...] * g
+        dk_own[...] = (dm * val[...].astype(f32)).astype(bf16)
+        dv_own[...] = (dm * key[...].astype(f32)).astype(bf16)
+        for n, (src, dst) in enumerate([(dq_own, dq), (dk_own, dk), (dv_own, dv)]):
+            copy = pltpu.make_async_copy(src, dst, loc.at[n])
+            copy.start()
+            done.append(copy)
+
+    def out_near():
+        for _ in rounds["w"]:
+            pass
+        got_one(WC.at[:, lanes(other, c)], 5)
+        acc_ref[...] = out_part(0, near, None)
+
+    def out_far():
+        acc = out_part(near, CHIPS, acc_ref[...])
+        out_all[mine, :] = jnp.where(is_first, acc[:, :c], acc[:, c:]).astype(bf16)
+        out_send[...] = jnp.where(is_first, acc[:, c:], acc[:, :c]).astype(bf16)
+        links.send(out_send, out_all.at[mine], one_s.at[6], one_r.at[6], mate)
+
+    tasks = {
+        "p0": product_near, "p1": product_far, "bs": back_states, "be": back_start,
+        "b": back_piece, "bz": back_end, "o0": out_near, "o1": out_far,
+    }
+    for name in SCHEDULE:
+        if name in tasks:
+            tasks[name]()
+        elif name[0] == "g":
+            weight_part(int(name[1]))
+        elif name[0] == "f":
+            first.wave(int(name[1]))
+        elif name[0] == "s":
+            second.wave(int(name[1]))
+        else:
+            for one in name[1:]:
+                next(rounds[one], None)
+    for one in rounds.values():
+        for _ in one:
+            pass
     for n in range(1, count):
         here = small_all.at[ring.at(0, -n)]
         links.copy(here, here, sm_s.at[n], sm_r.at[n], mate).wait_recv()
@@ -514,23 +572,49 @@
     for n in range(1, count):
         total = total + small_all[n]
     small_sum[...] = total
-    done[3].start()
     got_one(out_all.at[its], 6)
-    done[4].start()
+    for n, (src, dst) in enumerate([(small_sum, small), (out_all, out)]):
+        copy = pltpu.make_async_copy(src, dst, loc.at[3 + n])
+        copy.start()
+        done.append(copy)
     links.drain()
     for copy in done:
         copy.wait()
 
 
-def finish(out_in, dq_in, dk_in, dv_in, small, dw_in, out, dq, dk, dv, dres, drate, dskip, dw):
-    out[...] = out_in[...]
-    dq[...] = dq_in[...]
-    dk[...] = dk_in[...]
-    dv[...] = dv_in[...]
+def finish(out_in, dq_in, dk_in, dv_in, small, dw_in, out, dq, dk, dv, dres, drate, dskip, dw, thin, taken, given, sems):
+    runs = 4
+    rows = taken.shape[0] // runs
+    parts = [pl.ds(n * rows, rows) for n in range(runs)]
+    wide_in = [
+        pltpu.make_async_copy(dw_in.at[part], taken.at[part], sems.at[0, n])
+        for n, part in enumerate(parts)
+    ]
+    thin_in = [
+        pltpu.make_async_copy(src, thin.at[n], sems.at[1, n])
+        for n, src in enumerate((out_in, dq_in, dk_in, dv_in))
+    ]
+    wide_out = [
+        pltpu.make_async_copy(given.at[part], dw.at[part], sems.at[2, n])
+        for n, part in enumerate(parts)
+    ]
+    thin_out = [
+        pltpu.make_async_copy(thin.at[n], dst, sems.at[3, n])
+        for n, dst in enumerate((out, dq, dk, dv))
+    ]
+    for copy in wide_in + thin_in:
+        copy.start()
     dres[...] = small[:MODES]
     drate[...] = small[MODES : 2 * MODES]
     dskip[...] = small[2 * MODES : 2 * MODES + 1]
-    dw[...] = dw_in[...].astype(f32)
+    for n, part in enumerate(parts):
+        wide_in[n].wait()
+        given[part, :] = taken[part, :].astype(f32)
+        wide_out[n].start()
+        thin_in[n].wait()
+        thin_out[n].start()
+    for copy in wide_out + thin_out:
+        copy.wait()
 
 
 def shards(queries, keys, values, residue, rate, skip, w_out, lengths, d_out):
@@ -552,11 +636,12 @@
         vmem((2, MODES, c), f32), vmem((2, 3, MODES, c), f32), vmem((count, rows, c), f32),
         vmem((rows, c), f32),
         vmem((c, n_out), f32), vmem((c, n_out), bf16), vmem((c, n_out), bf16),
-        vmem((2, LOTS, far + 1, c // LOTS, n_out // count), bf16), vmem((c, n_out), bf16),
-        dma((STREAMS, CHIPS, 2)), dma((STREAMS, CHIPS)), dma((STREAMS, CHIPS, 2)),
-        dma((STREAMS, CHIPS)), dma((9,)), dma((7,)), dma((7,)), dma((CHIPS,)), dma((CHIPS,)),
+        vmem((3, 2, 2, far + 1, c // count, 3 * wide), bf16), vmem((c, n_out), bf16),
+        dma((2, len(KEYS))), dma((2, len(KEYS))), dma((2, len(KEYS))), dma((2, len(KEYS))),
+        dma((9,)), dma((10,)), dma((10,)), dma((CHIPS,)), dma((CHIPS,)),
         dma((2, 2, far)), dma((2, 2, far)), dma((2, 3)), dma((2, 3)), dma((count,)), dma((count,)),
-        dma((2, LOTS, far)), dma((2, LOTS, far)), dma((2, LOTS, far)), dma((2, LOTS, far)),
+        dma((3, 2, 2, far)), dma((3, 2, 2, far)), dma((3, 2, 2, far)), dma((3, 2, 2, far)),
+        vmem((half, wide), f32), dma((CHIPS,)),
     ]
     whole = pl.BlockSpec(memory_space=pltpu.VMEM)
     apart = pl.BlockSpec(memory_space=pl.ANY)
@@ -580,8 +665,11 @@
             thin, thin, thin, thin, state, state, jax.ShapeDtypeStruct((1, c), f32),
             jax.ShapeDtypeStruct((c, n_out), f32),
         ),
-        in_specs=[whole] * 6,
-        out_specs=(whole,) * 8,
+        in_specs=[apart] * 4 + [whole, apart],
+        out_specs=(apart,) * 4 + (whole,) * 3 + (apart,),
+        scratch_shapes=[
+            vmem((4, t, c), bf16), vmem((c, n_out), bf16), vmem((c, n_out), f32), dma((4, 4)),
+        ],
         compiler_params=pltpu.CompilerParams(vmem_limit_bytes=60 * MIB),
     )(out, dq, dk, dv, small, dw)
     return out, dq, dk, dv, dres.T, drate.T, dskip[0], dw

time: 94.4 us -> 88.5 us (0.937)
  Pallas kernels: 92.9 us -> 87.7 us
    pallas_call x1, Pallas kernels: 89.6 us -> 83.4 us  [shards(): pl.pallas_call(functools.partial(kernel, count), out_shape=(thin, thin, t...]
    pallas_call x1, Pallas kernels: 3.27 us -> 4.22 us  [shards(): pl.pallas_call(finish, out_shape=(thin, thin, thin, thin, state, state, j...]
where the time goes in v4:
time: 88.5 us; the launch traced here: 88.3 us
  Pallas kernels  87.7 us (99%)
    pallas_call x1, Pallas kernels, shards(): pl.pallas_call(functools.partial(kernel, count), out_shape=(thin, thin, t...  83.4 us
    pallas_call x1, Pallas kernels, shards(): pl.pallas_call(finish, out_shape=(thin, thin, thin, thin, state, state, j...  4.22 us

profile of v4, /device:TPU:1, one launch (start us, length us, event | category | flops | bytes accessed | tf_op | source)
XLA Modules:
  0.0 88.3 jit_solution(11643272659917523824)
XLA Ops:
  0.6 83.4 %shard_map.152 = (bf16[1024,128]{1,0:T(8,128)(2,1)}, bf16[1024,128]{1,0:T(8,128)(2,1)}, bf16[1024,128]{1,0:T(8,128)(2,1)}, bf16[1024,128]{1,0:T(8,128)(2,1)}, f3...) custom-call(s32[3]{0:T(128)} %lengths.1, bf16[1024,128]{1,0:T(8,128)(2,1)} %q_in.1, bf16[1024,128]{1,0:T(8,128)(2,1)} %key_in.1, ...), custom_call_target="tpu_custom_call" | custom-call | tf_op jit(solution)/shard_map/pallas_call | solution.py:648
  84.1 4.2 %shard_map.153 = (bf16[1024,128]{1,0:T(8,128)(2,1)}, bf16[1024,128]{1,0:T(8,128)(2,1)}, bf16[1024,128]{1,0:T(8,128)(2,1)}, bf16[1024,128]{1,0:T(8,128)(2,1)}, f3...) custom-call(bf16[1024,128]{1,0:T(8,128)(2,1)} %get-tuple-element.22.out_in, ...), custom_call_target="tpu_custom_call" | custom-call | tf_op jit(solution)/shard_map/pallas_call | solution.py:662

commit v5 on v4

--- a/solution.py
+++ b/solution.py
@@ -141,9 +141,9 @@
     KEYS += [(i, 1, FULL), (i, -1, FULL), (i, 2, LOW), (i, 2, HIGH)]
 OFFSETS = sorted([(i, j) for i in NEAR for j in NEAR], key=lambda o: abs(o[0]) + abs(o[1]))
 SCHEDULE = (
-    "tw", "g0", "f2", "t0w", "g1", "p0", "f3", "t01w", "s0", "f4", "g2", "p1", "t01w", "bs",
+    "tw", "g0", "f2", "t0w", "g1", "p0", "f3", "t01w", "s0", "f4", "g2", "p1", "t012w", "bs",
     "t012w", "s1", "be", "t012w", "b", "b", "t012w", "b", "b", "t012", "s2", "b", "bz", "t012",
-    "t012", "t012", "s3", "t012", "o0", "t012", "s4", "t012", "o1",
+    "t012", "s3", "t012", "o0", "t012", "s4", "t012", "o1",
 )
 GROUPS = [((0, 3), (3, 5)), ((5, 8), (8, 11)), ((11, 13), (13, 16))]
 
@@ -582,39 +582,15 @@
         copy.wait()
 
 
-def finish(out_in, dq_in, dk_in, dv_in, small, dw_in, out, dq, dk, dv, dres, drate, dskip, dw, thin, taken, given, sems):
-    runs = 4
-    rows = taken.shape[0] // runs
-    parts = [pl.ds(n * rows, rows) for n in range(runs)]
-    wide_in = [
-        pltpu.make_async_copy(dw_in.at[part], taken.at[part], sems.at[0, n])
-        for n, part in enumerate(parts)
-    ]
-    thin_in = [
-        pltpu.make_async_copy(src, thin.at[n], sems.at[1, n])
-        for n, src in enumerate((out_in, dq_in, dk_in, dv_in))
-    ]
-    wide_out = [
-        pltpu.make_async_copy(given.at[part], dw.at[part], sems.at[2, n])
-        for n, part in enumerate(parts)
-    ]
-    thin_out = [
-        pltpu.make_async_copy(thin.at[n], dst, sems.at[3, n])
-        for n, dst in enumerate((out, dq, dk, dv))
-    ]
-    for copy in wide_in + thin_in:
-        copy.start()
+def finish(out_in, dq_in, dk_in, dv_in, small, dw_in, out, dq, dk, dv, dres, drate, dskip, dw):
+    out[...] = out_in[...]
+    dq[...] = dq_in[...]
+    dk[...] = dk_in[...]
+    dv[...] = dv_in[...]
     dres[...] = small[:MODES]
     drate[...] = small[MODES : 2 * MODES]
     dskip[...] = small[2 * MODES : 2 * MODES + 1]
-    for n, part in enumerate(parts):
-        wide_in[n].wait()
-        given[part, :] = taken[part, :].astype(f32)
-        wide_out[n].start()
-        thin_in[n].wait()
-        thin_out[n].start()
-    for copy in wide_out + thin_out:
-        copy.wait()
+    dw[...] = dw_in[...].astype(f32)
 
 
 def shards(queries, keys, values, residue, rate, skip, w_out, lengths, d_out):
@@ -665,11 +641,8 @@
             thin, thin, thin, thin, state, state, jax.ShapeDtypeStruct((1, c), f32),
             jax.ShapeDtypeStruct((c, n_out), f32),
         ),
-        in_specs=[apart] * 4 + [whole, apart],
-        out_specs=(apart,) * 4 + (whole,) * 3 + (apart,),
-        scratch_shapes=[
-            vmem((4, t, c), bf16), vmem((c, n_out), bf16), vmem((c, n_out), f32), dma((4, 4)),
-        ],
+        in_specs=[whole] * 6,
+        out_specs=(whole,) * 8,
         compiler_params=pltpu.CompilerParams(vmem_limit_bytes=60 * MIB),
     )(out, dq, dk, dv, small, dw)
     return out, dq, dk, dv, dres.T, drate.T, dskip[0], dw

time: 88.5 us -> 85.9 us (0.971)
  Pallas kernels: 87.7 us -> 85.1 us
    pallas_call x1, Pallas kernels: 83.4 us -> 81.8 us  [shards(): pl.pallas_call(functools.partial(kernel, count), out_shape=(thin, thin, t...]
    pallas_call x1, Pallas kernels: 4.22 us -> 3.27 us  [shards(): pl.pallas_call(finish, out_shape=(thin, thin, thin, thin, state, state, j...]
where the time goes in v5:
time: 85.9 us; the launch traced here: 85.8 us
  Pallas kernels  85.1 us (99%)
    pallas_call x1, Pallas kernels, shards(): pl.pallas_call(functools.partial(kernel, count), out_shape=(thin, thin, t...  81.8 us
    pallas_call x1, Pallas kernels, shards(): pl.pallas_call(finish, out_shape=(thin, thin, thin, thin, state, state, j...  3.27 us

profile of v5, /device:TPU:1, one launch (start us, length us, event | category | flops | bytes accessed | tf_op | source)
XLA Modules:
  0.0 85.8 jit_solution(11554587539834148574)
XLA Ops:
  0.6 81.8 %shard_map.152 = (bf16[1024,128]{1,0:T(8,128)(2,1)}, bf16[1024,128]{1,0:T(8,128)(2,1)}, bf16[1024,128]{1,0:T(8,128)(2,1)}, bf16[1024,128]{1,0:T(8,128)(2,1)}, f3...) custom-call(s32[3]{0:T(128)} %lengths.1, bf16[1024,128]{1,0:T(8,128)(2,1)} %q_in.1, bf16[1024,128]{1,0:T(8,128)(2,1)} %key_in.1, ...), custom_call_target="tpu_custom_call" | custom-call | tf_op jit(solution)/shard_map/pallas_call | solution.py:624
  82.5 3.3 %shard_map.153 = (bf16[1024,128]{1,0:T(8,128)(2,1)}, bf16[1024,128]{1,0:T(8,128)(2,1)}, bf16[1024,128]{1,0:T(8,128)(2,1)}, bf16[1024,128]{1,0:T(8,128)(2,1)}, f3...) custom-call(bf16[1024,128]{1,0:T(8,128)(2,1)} %get-tuple-element.22.out_in, ...), custom_call_target="tpu_custom_call" | custom-call | tf_op jit(solution)/shard_map/pallas_call | solution.py:638

commit v6 on v5

--- a/solution.py
+++ b/solution.py
@@ -141,7 +141,7 @@
     KEYS += [(i, 1, FULL), (i, -1, FULL), (i, 2, LOW), (i, 2, HIGH)]
 OFFSETS = sorted([(i, j) for i in NEAR for j in NEAR], key=lambda o: abs(o[0]) + abs(o[1]))
 SCHEDULE = (
-    "tw", "g0", "f2", "t0w", "g1", "p0", "f3", "t01w", "s0", "f4", "g2", "p1", "t012w", "bs",
+    "tw", "g0", "f2", "t0w", "g1", "p0", "f3", "t01w", "s0", "f4", "g2", "t012w", "p1", "bs",
     "t012w", "s1", "be", "t012w", "b", "b", "t012w", "b", "b", "t012", "s2", "b", "bz", "t012",
     "t012", "s3", "t012", "o0", "t012", "s4", "t012", "o1",
 )

time: 85.9 us -> 86.9 us (1.012)
  Pallas kernels: 85.1 us -> 86.2 us
    pallas_call x1, Pallas kernels: 81.8 us -> 82.9 us  [shards(): pl.pallas_call(functools.partial(kernel, count), out_shape=(thin, thin, t...]
where the time goes in v6:
time: 86.9 us; the launch traced here: 86.8 us
  Pallas kernels  86.2 us (99%)
    pallas_call x1, Pallas kernels, shards(): pl.pallas_call(functools.partial(kernel, count), out_shape=(thin, thin, t...  82.9 us
    pallas_call x1, Pallas kernels, shards(): pl.pallas_call(finish, out_shape=(thin, thin, thin, thin, state, state, j...  3.27 us

profile of v6, /device:TPU:1, one launch (start us, length us, event | category | flops | bytes accessed | tf_op | source)
XLA Modules:
  0.0 86.8 jit_solution(12958777507119777904)
XLA Ops:
  0.6 82.9 %shard_map.152 = (bf16[1024,128]{1,0:T(8,128)(2,1)}, bf16[1024,128]{1,0:T(8,128)(2,1)}, bf16[1024,128]{1,0:T(8,128)(2,1)}, bf16[1024,128]{1,0:T(8,128)(2,1)}, f3...) custom-call(s32[3]{0:T(128)} %lengths.1, bf16[1024,128]{1,0:T(8,128)(2,1)} %q_in.1, bf16[1024,128]{1,0:T(8,128)(2,1)} %key_in.1, ...), custom_call_target="tpu_custom_call" | custom-call | tf_op jit(solution)/shard_map/pallas_call | solution.py:624
  83.6 3.3 %shard_map.153 = (bf16[1024,128]{1,0:T(8,128)(2,1)}, bf16[1024,128]{1,0:T(8,128)(2,1)}, bf16[1024,128]{1,0:T(8,128)(2,1)}, bf16[1024,128]{1,0:T(8,128)(2,1)}, f3...) custom-call(bf16[1024,128]{1,0:T(8,128)(2,1)} %get-tuple-element.22.out_in, ...), custom_call_target="tpu_custom_call" | custom-call | tf_op jit(solution)/shard_map/pallas_call | solution.py:638
